TPU v7x, 128 devices: a whole 4x4x4 slice. The times are simulated.
128 devices in a mesh: dp: 8 (over z, core), ctx: 16 (over y, x).
Axes of the slice: x: 4, y: 4, z: 4, core: 2. Of those that a mesh axis runs over, the one named last changes fastest.
Arguments:
- tokens: bfloat16 [24576, 1024], P(('dp', 'ctx')), may hold values from -55 to 55
- segments: int32 [8, 3072], P('dp', 'ctx'), may hold values from 0 to 7, never falling along the last dimension, each value on 1 to 1536 neighbouring positions
- w_in: bfloat16 [1024, 4096], replicated, may hold values from -0.1875 to 0.1875
- w_out: bfloat16 [1024, 1024], replicated, may hold values from -0.1875 to 0.1875
- grad_out: bfloat16 [24576, 1024], P(('dp', 'ctx')), may hold values from -24 to 24
Outputs:
- layer_out: bfloat16 [24576, 1024], P(('dp', 'ctx'))
- grad_tokens: bfloat16 [24576, 1024], P(('dp', 'ctx'))
- out_grad: float32 [1024, 1024], P(('dp', 'ctx'))
Inputs may be any that keep to these rules, and one draw needn't show every extreme that they name: `segments`: along each stream's stored rows the history number never falls; each of the 8 histories holds 1 to 1536 events, one exactly 1536.
All inputs are finite; a program needn't handle non-finite values.
Results may differ from a plain program's by a relative error of at most 0.008.
Values may be sent and summed in bfloat16 or wider, within the bound.
A program may use at most 128 MiB of HBM per device.

v0:
```python
import jax
import jax.numpy as jnp
from jax import lax
from jax.sharding import PartitionSpec as P

HEADS = 8


EPS = 1e-05


def silu_grad(value):
    sigmoid_v = jax.nn.sigmoid(value)
    return sigmoid_v * (1.0 + value * (1.0 - sigmoid_v))


def norm_rows(matrix):
    average = jnp.mean(matrix, axis=-1, keepdims=True)
    centred = matrix - average
    inverse = lax.rsqrt(jnp.mean(centred * centred, axis=-1, keepdims=True) + EPS)
    return (centred * inverse, inverse)


def norm_back(gradient, normed, inverse):
    first = jnp.mean(gradient, axis=-1, keepdims=True)
    second = jnp.mean(gradient * normed, axis=-1, keepdims=True)
    return (gradient - first - normed * second) * inverse


def head_major(matrix):
    return matrix.reshape(matrix.shape[0], HEADS, matrix.shape[1] // HEADS).transpose(1, 0, 2)


def row_major(stacked):
    return stacked.transpose(1, 0, 2).reshape(stacked.shape[1], stacked.shape[0] * stacked.shape[2])


def place_of(stored, own_rows, ctx_count):
    block = stored // own_rows
    inner = stored % own_rows
    half = own_rows // 2
    return jnp.where(
        inner < half, block * half + inner, (2 * ctx_count - 1 - block) * half + inner - half
    )


def on_device(tokens, segments, w_in, w_out, grad_out):
    own_rows, model_width = tokens.shape
    ctx_count = lax.axis_size("ctx")
    score_scale = (model_width // HEADS) ** (-0.5)
    device_pos = lax.axis_index("ctx")
    positions = place_of(
        device_pos * own_rows + jnp.arange(own_rows, dtype=jnp.int32), own_rows, ctx_count
    )
    history = segments[0]
    xfloat = tokens.astype(jnp.float32)
    normed, inv_x = norm_rows(xfloat)
    normed_b = normed.astype(jnp.bfloat16)
    preact = jnp.dot(normed_b, w_in, preferred_element_type=jnp.float32)
    act = jax.nn.silu(preact).astype(jnp.bfloat16)
    gate_u = act[:, :model_width]
    own_values = act[:, model_width : 2 * model_width]
    queries = act[:, 2 * model_width : 3 * model_width]
    own_keys = act[:, 3 * model_width :]
    keys_all, values_all, history_all = (
        lax.all_gather(own_keys, "ctx", axis=0, tiled=True),
        lax.all_gather(own_values, "ctx", axis=0, tiled=True),
        lax.all_gather(history, "ctx", axis=0, tiled=True),
    )
    places_all = place_of(jnp.arange(keys_all.shape[0], dtype=jnp.int32), own_rows, ctx_count)
    visible = (history[:, None] == history_all[None, :]) & (
        positions[:, None] >= places_all[None, :]
    )
    query_h = head_major(queries)
    keys_h = head_major(keys_all)
    values_h = head_major(values_all)

    def forward_head(operands):
        one_q, one_k, one_v = operands
        scores = jnp.dot(one_q, one_k.T, preferred_element_type=jnp.float32) * score_scale
        weights = jnp.where(visible, jax.nn.silu(scores), 0.0).astype(jnp.bfloat16)
        return jnp.dot(weights, one_v, preferred_element_type=jnp.float32)

    mixed = row_major(lax.map(forward_head, (query_h, keys_h, values_h)))
    mixed_n, inv_o = norm_rows(mixed)
    gated = (mixed_n * gate_u.astype(jnp.float32)).astype(jnp.bfloat16)
    layer_out = (jnp.dot(gated, w_out, preferred_element_type=jnp.float32) + xfloat).astype(
        jnp.bfloat16
    )
    total_rows = own_rows * lax.axis_size(("dp", "ctx"))
    out_grad = lax.psum_scatter(
        jnp.einsum("re,rd->ed", grad_out, gated, preferred_element_type=jnp.float32),
        ("dp", "ctx"),
        scatter_dimension=0,
        tiled=True,
    ) * total_rows ** (-0.5)
    grad_gated = jnp.einsum("re,de->rd", grad_out, w_out, preferred_element_type=jnp.float32)
    grad_u = grad_gated * mixed_n
    grad_norm = grad_gated * gate_u.astype(jnp.float32)
    grad_mixed = norm_back(grad_norm, mixed_n, inv_o).astype(jnp.bfloat16)
    grad_h = head_major(grad_mixed)

    def query_head(operands):
        one_q, one_k, one_v, one_g = operands
        scores = jnp.dot(one_q, one_k.T, preferred_element_type=jnp.float32) * score_scale
        grad_weights = jnp.dot(one_g, one_v.T, preferred_element_type=jnp.float32)
        grad_scores = (
            jnp.where(visible, grad_weights * silu_grad(scores), 0.0) * score_scale
        ).astype(jnp.bfloat16)
        return jnp.dot(grad_scores, one_k, preferred_element_type=jnp.float32)

    grad_queries = row_major(lax.map(query_head, (query_h, keys_h, values_h, grad_h)))
    own_keys_h = head_major(own_keys)
    own_values_h = head_major(own_values)
    piece_q = lax.all_gather(queries, "ctx", axis=0, tiled=True)
    piece_grad = lax.all_gather(grad_mixed, "ctx", axis=0, tiled=True)
    piece_hist = lax.all_gather(history, "ctx", axis=0, tiled=True)
    row_count = piece_q.shape[0]
    piece_pos = place_of(jnp.arange(row_count, dtype=jnp.int32), own_rows, ctx_count)
    piece_visible = (piece_hist[:, None] == history[None, :]) & (
        piece_pos[:, None] >= positions[None, :]
    )

    def key_head(operands):
        one_q, one_g, one_k, one_v = operands
        scores = jnp.dot(one_q, one_k.T, preferred_element_type=jnp.float32) * score_scale
        weights = jnp.where(piece_visible, jax.nn.silu(scores), 0.0).astype(jnp.bfloat16)
        grad_weights = jnp.dot(one_g, one_v.T, preferred_element_type=jnp.float32)
        grad_scores = (
            jnp.where(piece_visible, grad_weights * silu_grad(scores), 0.0) * score_scale
        ).astype(jnp.bfloat16)
        key_part = jnp.dot(grad_scores.T, one_q, preferred_element_type=jnp.float32)
        value_part = jnp.dot(weights.T, one_g, preferred_element_type=jnp.float32)
        return (key_part, value_part)

    key_part, value_part = lax.map(
        key_head, (head_major(piece_q), head_major(piece_grad), own_keys_h, own_values_h)
    )
    grad_keys = row_major(key_part)
    grad_values = row_major(value_part)
    grad_all = jnp.concatenate([grad_u, grad_values, grad_queries, grad_keys], axis=1)
    grad_pre = (grad_all * silu_grad(preact)).astype(jnp.bfloat16)
    grad_rows = jnp.einsum("rf,df->rd", grad_pre, w_in, preferred_element_type=jnp.float32)
    grad_tokens = (grad_out.astype(jnp.float32) + norm_back(grad_rows, normed, inv_x)).astype(
        jnp.bfloat16
    )
    return (layer_out, grad_tokens, out_grad)


def solution(mesh):
    return jax.shard_map(
        on_device,
        mesh=mesh,
        in_specs=(P(("dp", "ctx"), None), P("dp", "ctx"), P(), P(), P(("dp", "ctx"), None)),
        out_specs=(P(("dp", "ctx"), None), P(("dp", "ctx"), None), P(("dp", "ctx"), None)),
        check_vma=False,
    )
```

profile of v0, /device:TPU:1, one launch (start us, length us, event | category | flops | bytes accessed | tf_op | source)
XLA Modules:
  0.0 1003.1 jit_solution(6318163071438569828)
XLA Ops:
  9.8 7.2 multiply_convert_fusion
  23.6 62.2 %all-reduce = s32[3072]{0:T(1024)S(1)} all-reduce(s32[3072]{0:T(1024)S(1)} %dynamic-update-slice), channel_id=2, replica_groups=mesh['dp'=8,'ctx'=16] {'ctx'}, use_global_device_ids=true, to_apply=%add | all-reduce | flops 3072 | bytes 24576 | tf_op jit(solution)/shard_map/all_gather | solution.py:68
  85.8 6.6 bitcast_bitcast_fusion.2
  92.4 55.4 %all-gather.6.cloned.1.call-done = bf16[3072,1024]{1,0:T(8,128)(2,1)} async-done(((bf16[192,1024]{1,0:T(8,128)(2,1)}), bf16[3072,1024]{1,0:T(8,128)(2,1)}) %all-gather.6.cloned.1.call-update) | async-done | bytes 6291472 | tf_op jit(solution)/shard_map/all_gather | solution.py:66
  147.8 6.5 bitcast_bitcast_fusion.3
  154.4 22.1 %while.35 = (s32[]{:T(128)}, f32[8,192,128]{2,1,0:T(8,128)S(1)}, bf16[8,192,128]{2,1,0:T(8,128)(2,1)}, bf16[8,3072,128]{2,1,0:T(8,128)(2,1)}, bf16[8,3072,128]{2...) while((s32[]{:T(128)}, f32[8,192,128]{2,1,0:T(8,128)S(1)}, ...), condition=%wide.region_3.4_spmd.clone, body=%wide.region_2.3_spmd.clone.sunk | while | flops 307888128 | bytes 1749093 | solution.py:84
  176.8 3.8 convolution_bitcast_fusion
  180.6 5.4 copy.34
  195.5 58.9 %while.37 = (s32[]{:T(128)}, f32[8,192,128]{2,1,0:T(8,128)}, bf16[8,192,128]{2,1,0:T(8,128)(2,1)}, bf16[8,3072,128]{2,1,0:T(8,128)(2,1)}, bf16[8,192,128]{2,1,0:...) while((s32[]{:T(128)}, f32[8,192,128]{2,1,0:T(8,128)}, ...), condition=%wide.region_11.12_spmd.clone, body=%wide.region_10.11_spmd.clone.sunk | while | flops 461832192 | bytes 7303789 | solution.py:112
  195.5 3.1 convolution_multiply_fusion.8
  198.6 4.4 fusion.202
  206.0 4.3 fusion.202
  213.3 4.3 fusion.202
  220.7 4.3 fusion.202
  228.0 4.3 fusion.202
  235.4 4.3 fusion.202
  242.7 4.3 fusion.202
  250.1 4.3 fusion.202
  258.9 6.6 bitcast_bitcast_fusion
  265.5 559.4 %reduce-scatter.4.cloned.1.call-done = f32[8,1024]{1,0:T(8,128)} async-done(((f32[1024,1024]{1,0:T(8,128)}), f32[8,1024]{1,0:T(8,128)}) %reduce-scatter.4.cloned.1.call-update) | async-done | bytes 32784
  826.6 87.1 %all-gather.10.cloned.1.call-done = bf16[3072,1024]{1,0:T(8,128)(2,1)} async-done(((bf16[192,1024]{1,0:T(8,128)(2,1)}), bf16[3072,1024]{1,0:T(8,128)(2,1)}) %all-gather.10.cloned.1.call-update) | async-done | bytes 6291472 | tf_op jit(solution)/shard_map/all_gather | solution.py:116
  913.7 6.6 bitcast_bitcast_fusion.1
  922.3 63.1 %while.36 = (s32[]{:T(128)}, f32[8,192,128]{2,1,0:T(8,128)}, f32[8,192,128]{2,1,0:T(8,128)}, bf16[8,3072,128]{2,1,0:T(8,128)(2,1)}, bf16[8,192,128]{2,1,0:T(8,12...) while((s32[]{:T(128)}, f32[8,192,128]{2,1,0:T(8,128)}, ...), condition=%wide.region_9.10_spmd.clone, body=%wide.region_8.9_spmd.clone.sunk | while | flops 618135552 | bytes 10574965 | solution.py:136
  923.9 3.6 fusion.195
  931.8 3.6 fusion.195
  939.6 3.6 fusion.195
  947.6 3.6 fusion.195
  955.4 3.6 fusion.195
  963.3 3.6 fusion.195
  971.2 3.6 fusion.195
  979.1 3.6 fusion.195
  988.0 7.4 fusion.148
  (99 shorter events, 107.6 us)
Async XLA Ops:
  7.2 179.0 %copy-start = (bf16[1024,1024]{1,0:T(8,128)(2,1)S(1)}, bf16[1024,1024]{1,0:T(8,128)(2,1)}, u32[]{:S(2)}) copy-start(bf16[1024,1024]{1,0:T(8,128)(2,1)} %param.14) | copy-start | bytes 6291460
  7.2 78.6 %all-gather.8.cloned.1.call-start = ((), (), s32[]{:S(2)}) async-start(), calls=%async_computation.2 | async-start | bytes 6684672 | tf_op jit(solution)/shard_map/all_gather | solution.py:67
  16.9 1.1 copy-start.3
  18.1 3.8 copy-start.10
  18.1 5.2 copy-start.9
  19.5 128.3 %all-gather.6.cloned.1.call-start = ((), (), s32[]{:S(2)}) async-start(), calls=%async_computation.1 | async-start | bytes 6684672 | tf_op jit(solution)/shard_map/all_gather | solution.py:66
  20.3 238.6 %all-gather.12.cloned.1.call-start = ((), (), s32[]{:S(2)}) async-start(), calls=%async_computation.4 | async-start | bytes 6684672 | tf_op jit(solution)/shard_map/all_gather | solution.py:115
  21.0 803.8 %reduce-scatter.4.cloned.1.call-start = ((), (), s32[]{:S(2)}) async-start(), calls=%async_computation.5 | async-start | bytes 4227072
  154.4 22.5 %copy-start.4 = (bf16[192,1024]{1,0:T(8,128)(2,1)S(1)}, bf16[192,1024]{1,0:T(8,128)(2,1)}, u32[]{:S(2)}) copy-start(bf16[192,1024]{1,0:T(8,128)(2,1)} %param.15) | copy-start | bytes 1179652
  186.1 727.7 %all-gather.10.cloned.1.call-start = ((), (), s32[]{:S(2)}) async-start(), calls=%async_computation.3 | async-start | bytes 6684672 | tf_op jit(solution)/shard_map/all_gather | solution.py:116
  188.2 2.4 copy-start.6
  195.5 61.0 %copy-start.2 = (bf16[192,1024]{1,0:T(8,128)(2,1)S(1)}, bf16[192,1024]{1,0:T(8,128)(2,1)}, u32[]{:S(2)}) copy-start(bf16[192,1024]{1,0:T(8,128)(2,1)} %param.11) | copy-start | bytes 1179652
  985.4 2.6 copy-start.7
  985.4 2.6 copy-start.8
  987.9 7.5 copy-start.5
  988.0 8.6 copy-start.1
Sparse Core Ops, SparseCore 0:
  19.6 65.2 all-gather.7
  87.0 60.7 all-gather.5
  149.9 60.8 all-gather.11
  213.0 611.7 reduce-scatter.3
  827.0 86.6 all-gather.9
where the time goes:
time: 1010 us; the launch traced here: 1000 us
  waiting for transfers between devices  703 us (70%)
  matrix products  167 us (17%)
  blocking collectives  62.2 us (6%)
  local copies, waits for them, and re-layouts  49.4 us (5%)
  between operations  14.7 us (1%)
    unnamed x6, waiting for transfers between devices  561 us
    all_gather x1, waiting for transfers between devices, on_device(): piece_grad = lax.all_gather(grad_mixed, 'ctx', axis=0, tiled=True)  87.1 us
    all_gather x1, blocking collectives, on_device(): lax.all_gather(history, 'ctx', axis=0, tiled=True)  62.2 us
    all_gather x1, waiting for transfers between devices, on_device(): lax.all_gather(own_keys, 'ctx', axis=0, tiled=True)  55.4 us
    dot_general x8, matrix products, query_head(): return jnp.dot(grad_scores, one_k, preferred_element_type=jnp.float32)  34.5 us
    transpose x6, local copies, waits for them, and re-layouts, head_major(): matrix.reshape(matrix.shape[0], HEADS, matrix.shape[1] // HEADS)  30.2 us
    dot_general x8, matrix products, key_head(): key_part = jnp.dot(grad_scores.T, one_q, preferred_element_type=jnp.float32)  28.8 us
    dot_general x8, matrix products, query_head(): jnp.dot(one_q, one_k.T, preferred_element_type=jnp.float32) * score_scale  24.4 us
  transfers between devices with their start and end apart: 5, of which 3 were waited for; matrix products, arithmetic and copies ran while one was open for 13% of the time, Pallas kernels for 0%

commit v1 on v0

v1 whole, which is shorter than its diff:
```python
import functools

import jax
import jax.numpy as jnp
from jax import lax
from jax.experimental import pallas as pl
from jax.experimental.pallas import tpu as pltpu
from jax.sharding import PartitionSpec as P

HEADS = 8
HEAD = 128
ROWS = 192
HALF = 96
D = 1024
CTX = 16
EPS = 1e-05
SCALE = HEAD ** (-0.5)
VMEM_LIMIT = 56 * 1024 * 1024
F32 = jnp.float32
BF16 = jnp.bfloat16
K_COL, V_COL, Q_COL, U_COL = 3 * D, D, 2 * D, 0


def silu_and_grad(value):
    half = 0.5 * value
    tanh_h = jnp.tanh(half)
    sigmoid_v = 0.5 + 0.5 * tanh_h
    silu_v = half + half * tanh_h
    return silu_v, sigmoid_v + silu_v * (1.0 - sigmoid_v)


def norm_rows(matrix):
    average = jnp.mean(matrix, axis=-1, keepdims=True)
    centred = matrix - average
    inverse = lax.rsqrt(jnp.mean(centred * centred, axis=-1, keepdims=True) + EPS)
    return centred * inverse, inverse


def norm_back(gradient, normed, inverse):
    first = jnp.mean(gradient, axis=-1, keepdims=True)
    second = jnp.mean(gradient * normed, axis=-1, keepdims=True)
    return (gradient - first - normed * second) * inverse


def dot_nt(left, right):
    return lax.dot_general(left, right, (((1,), (1,)), ((), ())), preferred_element_type=F32)


def dot_tn(left, right):
    return lax.dot_general(left, right, (((0,), (0,)), ((), ())), preferred_element_type=F32)


def dot_nn(left, right):
    return lax.dot_general(left, right, (((1,), (0,)), ((), ())), preferred_element_type=F32)


class Place:
    def __init__(self):
        self.dp = lax.axis_index("dp")
        self.t = lax.axis_index("ctx")
        self.plane = 2 * (self.dp // 2)
        self.core = self.dp % 2
        self.sibling = {"dp": self.plane + 1 - self.core}

    def worker(self, head):
        return self.plane + self.t % 2, self.core * HEADS + head

    def owner(self, i):
        return self.plane + self.t // HEADS, 2 * i + self.core

    def is_me(self, device):
        return (device[0] == self.dp) & (device[1] == self.t)


def ident(device):
    return {"dp": device[0], "ctx": device[1]}


def signal_if_other(place, barrier, device):
    @pl.when(jnp.logical_not(place.is_me(device)))
    def _():
        pl.semaphore_signal(barrier, inc=1, device_id=ident(device))


def start_copy(place, device, src, dst, send_sem, recv_sem):
    mine = place.is_me(device)

    @pl.when(mine)
    def _():
        pltpu.make_async_copy(src, dst, recv_sem).start()

    @pl.when(jnp.logical_not(mine))
    def _():
        pltpu.make_async_remote_copy(
            src, dst, send_sem, recv_sem, device_id=ident(device)
        ).start()


def wait_sent(place, device, src, dst, send_sem, recv_sem):
    @pl.when(jnp.logical_not(place.is_me(device)))
    def _():
        pltpu.make_async_remote_copy(
            src, dst, send_sem, recv_sem, device_id=ident(device)
        ).wait_send()


def wait_arrived(dst, recv_sem):
    pltpu.make_async_copy(dst, dst, recv_sem).wait()


def project_kernel(
    tokens, hist, w_in, q_got, kv_got, hist_all, u_act, preact_out,
    w_buf, normed_buf, pre_buf, u_buf, send_buf, hist_buf,
    w_sem, out_sem, send_sem, recv_sem, fsend, frecv, hsend, hrecv, hfsend, hfrecv,
):
    place = Place()
    chunks = [K_COL, K_COL + 512, V_COL, V_COL + 512, Q_COL, Q_COL + 512, U_COL, U_COL + 512]

    def w_copy(n):
        cols = pl.ds(chunks[n], 512)
        return pltpu.make_async_copy(w_in.at[:, cols], w_buf.at[:, cols], w_sem.at[n])

    for n in range(8):
        w_copy(n).start()

    barrier = pltpu.get_barrier_semaphore()
    for i in range(8):
        signal_if_other(place, barrier, place.owner(i))
    pl.semaphore_signal(barrier, inc=1, device_id=place.sibling)

    normed, _ = norm_rows(tokens[...].astype(F32))
    normed_buf[...] = normed.astype(BF16)
    hist_buf[...] = jnp.zeros_like(hist_buf)
    hist_buf[:, 0:HALF] = hist[:, 0:HALF]
    hist_buf[:, 128 : 128 + HALF] = hist[:, HALF:ROWS]

    self_work = (place.t % 2 == place.core) & (place.t // HEADS == place.core)
    expected = 9 - self_work.astype(jnp.int32)
    pl.semaphore_wait(barrier, expected)

    slot = place.t // 2

    def send_args(kind, head):
        src = send_buf.at[kind, head]
        if kind == 2:
            dst = q_got.at[slot]
        else:
            dst = kv_got.at[kind, :, place.t]
        return place.worker(head), src, dst, send_sem.at[kind, head], recv_sem.at[kind, slot]

    def hist_args(head):
        return (
            place.worker(head), hist_buf, hist_all.at[place.t], hsend.at[head], hrecv.at[slot],
        )

    for head in range(HEADS):
        start_copy(place, *hist_args(head))

    for n in range(8):
        w_copy(n).wait()
        cols = slice(chunks[n], chunks[n] + 512)
        pre = dot_nn(normed_buf[...], w_buf[:, cols])
        pre_buf[:, cols] = pre
        half = 0.5 * pre
        act = (half + half * jnp.tanh(half)).astype(BF16)
        if n < 6:
            kind = n // 2
            for j in range(4):
                head = (n % 2) * 4 + j
                send_buf[kind, head] = act[:, j * 128 : (j + 1) * 128].reshape(2, HALF, HEAD)
                start_copy(place, *send_args(kind, head))
        else:
            u_buf[:, cols] = act

    u_out = pltpu.make_async_copy(u_buf, u_act, out_sem.at[0])
    u_out.start()
    p_out = pltpu.make_async_copy(pre_buf, preact_out, out_sem.at[1])
    p_out.start()

    def forward(kind, i):
        c = 2 * i + place.core
        ref = kv_got.at[kind, :, c]
        return pltpu.make_async_remote_copy(
            ref, ref, fsend.at[kind, i], frecv.at[kind, i], device_id=place.sibling
        )

    def hforward(i):
        c = 2 * i + place.core
        return pltpu.make_async_remote_copy(
            hist_all.at[c], hist_all.at[c], hfsend.at[i], hfrecv.at[i], device_id=place.sibling
        )

    for i in range(8):
        wait_arrived(hist_all.at[2 * i + place.core], hrecv.at[i])
        hforward(i).start()
    for kind in range(2):
        for i in range(8):
            wait_arrived(kv_got.at[kind, :, 2 * i + place.core], recv_sem.at[kind, i])
            forward(kind, i).start()
    for i in range(8):
        wait_arrived(q_got.at[i], recv_sem.at[2, i])
    for i in range(8):
        other = 2 * i + 1 - place.core
        wait_arrived(hist_all.at[other], hfrecv.at[i])
        for kind in range(2):
            wait_arrived(kv_got.at[kind, :, other], frecv.at[kind, i])
    for i in range(8):
        hforward(i).wait_send()
        for kind in range(2):
            forward(kind, i).wait_send()
    for head in range(HEADS):
        wait_sent(place, *hist_args(head))
        for kind in range(3):
            wait_sent(place, *send_args(kind, head))
    u_out.wait()
    p_out.wait()


def project(tokens, hist, w_in):
    any_spec = pl.BlockSpec(memory_space=pl.ANY)
    vmem_spec = pl.BlockSpec(memory_space=pltpu.VMEM)
    dma = pltpu.SemaphoreType.DMA
    return pl.pallas_call(
        project_kernel,
        out_shape=(
            jax.ShapeDtypeStruct((8, 2, HALF, HEAD), BF16),
            jax.ShapeDtypeStruct((2, 2, CTX, HALF, HEAD), BF16),
            jax.ShapeDtypeStruct((CTX, 1, 256), jnp.int32),
            jax.ShapeDtypeStruct((ROWS, D), BF16),
            jax.ShapeDtypeStruct((ROWS, 4 * D), F32),
        ),
        in_specs=[vmem_spec, vmem_spec, any_spec],
        out_specs=(any_spec,) * 5,
        scratch_shapes=[
            pltpu.VMEM((D, 4 * D), BF16),
            pltpu.VMEM((ROWS, D), BF16),
            pltpu.VMEM((ROWS, 4 * D), F32),
            pltpu.VMEM((ROWS, D), BF16),
            pltpu.VMEM((3, HEADS, 2, HALF, HEAD), BF16),
            pltpu.VMEM((1, 256), jnp.int32),
            dma((8,)), dma((2,)), dma((3, 8)), dma((3, 8)), dma((2, 8)), dma((2, 8)),
            dma((8,)), dma((8,)), dma((8,)), dma((8,)),
        ],
        compiler_params=pltpu.CompilerParams(
            collective_id=0, has_side_effects=True, vmem_limit_bytes=VMEM_LIMIT
        ),
        name="project_and_send",
    )(tokens, hist, w_in)


def column_of(row):
    wide = jnp.broadcast_to(row, (128, 128))
    on_diag = lax.broadcasted_iota(jnp.int32, (128, 128), 0) == lax.broadcasted_iota(
        jnp.int32, (128, 128), 1
    )
    return jnp.sum(jnp.where(on_diag, wide, 0), axis=1, keepdims=True)


def block_range(hist_s, first_block, last_block):
    first = hist_s[first_block, 0, 0]
    last = hist_s[last_block, 0, 128 + HALF - 1]
    low = jnp.int32(0)
    high = jnp.int32(CTX - 1)
    for c in range(CTX):
        low = low + (hist_s[c, 0, 128 + HALF - 1] < first).astype(jnp.int32)
        high = high - (hist_s[c, 0, 0] > last).astype(jnp.int32)
    return low, high


def lane_rows(hist_v, half, block, count):
    return [hist_v[block + n, :, half * 128 : half * 128 + HALF] for n in range(count)]


def attend_kernel(core_s, hist_s, hist_v, q_ref, kv_ref, out_ref, acc, row_f, hcol):
    core = core_s[0]
    for half in range(2):
        for group in range(4):
            row_f[half, group] = jnp.concatenate(lane_rows(hist_v, half, group * 4, 4), axis=1)

    def q_tile(tile, _):
        block_a = 4 * tile + core
        block_b = block_a + 2
        low, high = block_range(hist_s, block_a, block_b)
        for half in range(2):
            for n, block in enumerate((block_a, block_b)):
                col = column_of(hist_v[block, :, half * 128 : half * 128 + 128])
                hcol[n * HALF : (n + 1) * HALF] = col[:HALF]
            history = hcol[...]
            queries = jnp.concatenate([q_ref[2 * tile, half], q_ref[2 * tile + 1, half]], axis=0)
            acc[...] = jnp.zeros_like(acc)
            inner = lax.broadcasted_iota(jnp.int32, (ROWS, 1), 0)
            second = inner >= HALF
            q_block = jnp.where(second, block_b, block_a)
            q_in = jnp.where(second, inner - HALF, inner)
            q_pos = (31 - q_block if half else q_block) * HALF + q_in

            def step(group, k_half):
                keys = kv_ref[0, k_half, pl.ds(group * 4, 4)].reshape(4 * HALF, HEAD)
                values = kv_ref[1, k_half, pl.ds(group * 4, 4)].reshape(4 * HALF, HEAD)
                h = dot_nt(queries, keys) * (0.5 * SCALE)
                weights = h + h * jnp.tanh(h)
                visible = history == row_f[k_half, group]
                if half == k_half:
                    lane = lax.broadcasted_iota(jnp.int32, (1, 4 * HALF), 1)
                    inside = lane // HALF
                    k_block = group * 4 + inside
                    k_pos = (31 - k_block if half else k_block) * HALF + lane - inside * HALF
                    visible = visible & (k_pos <= q_pos)
                weights = jnp.where(visible, weights, 0.0).astype(BF16)
                acc[...] += dot_nn(weights, values)

            if half == 0:

                @pl.loop(low // 4, jnp.minimum(high, block_b) // 4 + 1)
                def _(group):
                    step(group, 0)
            else:

                @pl.loop(low // 4, high // 4 + 1)
                def _(group):
                    step(group, 0)

                @pl.loop(jnp.maximum(low, block_a) // 4, high // 4 + 1)
                def _(group):
                    step(group, 1)

            out_ref[2 * tile, half] = acc[0:HALF].astype(BF16)
            out_ref[2 * tile + 1, half] = acc[HALF:ROWS].astype(BF16)
        return 0

    lax.fori_loop(0, 4, q_tile, 0)


def attend(core, hist_all, q_got, kv_got):
    vmem_spec = pl.BlockSpec(memory_space=pltpu.VMEM)
    smem_spec = pl.BlockSpec(memory_space=pltpu.SMEM)
    return pl.pallas_call(
        attend_kernel,
        out_shape=jax.ShapeDtypeStruct((8, 2, HALF, HEAD), BF16),
        in_specs=[smem_spec, smem_spec, vmem_spec, vmem_spec, vmem_spec],
        out_specs=vmem_spec,
        scratch_shapes=[
            pltpu.VMEM((ROWS, HEAD), F32),
            pltpu.VMEM((2, 4, 1, 4 * HALF), jnp.int32),
            pltpu.VMEM((ROWS, 1), jnp.int32),
        ],
        compiler_params=pltpu.CompilerParams(vmem_limit_bytes=VMEM_LIMIT),
        name="attend",
    )(core, hist_all, hist_all, q_got, kv_got)


def middle_kernel(
    o_ref, tokens, u_act, grad_out, w_out, layer_out, do_got, gated_out, grad_u_out,
    mixed_got, send_buf, gate_buf, osend, orecv, gsend, grecv,
):
    place = Place()
    barrier = pltpu.get_barrier_semaphore()
    for n in range(8):
        signal_if_other(place, barrier, place.owner(n))
        signal_if_other(place, barrier, place.worker(n))
    self_work = (place.t % 2 == place.core) & (place.t // HEADS == place.core)
    pl.semaphore_wait(barrier, 16 - 2 * self_work.astype(jnp.int32))
    my_head = place.t % HEADS
    slot = place.t // 2

    def o_args(i):
        return (
            place.owner(i), o_ref.at[i], mixed_got.at[my_head], osend.at[i], orecv.at[my_head],
        )

    def g_args(head):
        return (
            place.worker(head), send_buf.at[head], do_got.at[slot], gsend.at[head], grecv.at[slot],
        )

    for i in range(8):
        start_copy(place, *o_args(i))
    grad_gated = dot_nt(grad_out[...], w_out[...])
    gate_buf[...] = grad_gated
    for head in range(HEADS):
        wait_arrived(mixed_got.at[head], orecv.at[head])
    mixed = jnp.concatenate(
        [mixed_got[head].reshape(ROWS, HEAD) for head in range(HEADS)], axis=1
    ).astype(F32)
    mixed_n, inv_o = norm_rows(mixed)
    gate_u = u_act[...].astype(F32)
    grad_gated = gate_buf[...]
    grad_mixed = norm_back(grad_gated * gate_u, mixed_n, inv_o).astype(BF16)
    for head in range(HEADS):
        send_buf[head] = grad_mixed[:, head * 128 : (head + 1) * 128].reshape(2, HALF, HEAD)
        start_copy(place, *g_args(head))
    grad_u_out[...] = grad_gated * mixed_n
    gated = (mixed_n * gate_u).astype(BF16)
    gated_out[...] = gated
    layer_out[...] = (dot_nn(gated, w_out[...]) + tokens[...].astype(F32)).astype(BF16)
    for i in range(8):
        wait_arrived(do_got.at[i], grecv.at[i])
    for n in range(8):
        wait_sent(place, *o_args(n))
        wait_sent(place, *g_args(n))


def middle(o_loc, tokens, u_act, grad_out, w_out):
    any_spec = pl.BlockSpec(memory_space=pl.ANY)
    vmem_spec = pl.BlockSpec(memory_space=pltpu.VMEM)
    dma = pltpu.SemaphoreType.DMA
    return pl.pallas_call(
        middle_kernel,
        out_shape=(
            jax.ShapeDtypeStruct((ROWS, D), BF16),
            jax.ShapeDtypeStruct((8, 2, HALF, HEAD), BF16),
            jax.ShapeDtypeStruct((ROWS, D), BF16),
            jax.ShapeDtypeStruct((ROWS, D), F32),
        ),
        in_specs=[vmem_spec] * 5,
        out_specs=(vmem_spec, any_spec, vmem_spec, vmem_spec),
        scratch_shapes=[
            pltpu.VMEM((HEADS, 2, HALF, HEAD), BF16),
            pltpu.VMEM((HEADS, 2, HALF, HEAD), BF16),
            pltpu.VMEM((ROWS, D), F32),
            dma((8,)), dma((8,)), dma((8,)), dma((8,)),
        ],
        compiler_params=pltpu.CompilerParams(
            collective_id=1, has_side_effects=True, vmem_limit_bytes=VMEM_LIMIT
        ),
        name="gate_and_send",
    )(o_loc, tokens, u_act, grad_out, w_out)


def attend_back_kernel(
    core_s, hist_s, hist_v, q_ref, kv_ref, do_ref, dq_ref, dkv_ref, dkv_acc, dq_acc, kcol, qrow
):
    core = core_s[0]
    dkv_acc[...] = jnp.zeros_like(dkv_acc)
    for half in range(2):
        for c in range(CTX):
            col = column_of(hist_v[c, :, half * 128 : half * 128 + 128])
            kcol[half, c // 2, (c % 2) * HALF : (c % 2 + 1) * HALF] = col[:HALF]

    def q_tile(tile, _):
        blocks = [8 * tile + 2 * n + core for n in range(4)]
        low, high = block_range(hist_s, blocks[0], blocks[3])
        for half in range(2):
            history = jnp.concatenate(
                [hist_v[block, :, half * 128 : half * 128 + HALF] for block in blocks], axis=1
            )
            qrow[...] = history
            queries = q_ref[pl.ds(4 * tile, 4), half].reshape(4 * HALF, HEAD)
            grads = do_ref[pl.ds(4 * tile, 4), half].reshape(4 * HALF, HEAD)
            dq_acc[...] = jnp.zeros_like(dq_acc)
            lane = lax.broadcasted_iota(jnp.int32, (1, 4 * HALF), 1)
            inside = lane // HALF
            q_block = blocks[0] + 2 * inside
            q_pos = (31 - q_block if half else q_block) * HALF + lane - inside * HALF

            def step(group, k_half):
                keys = kv_ref[0, k_half, pl.ds(group * 2, 2)].reshape(2 * HALF, HEAD)
                values = kv_ref[1, k_half, pl.ds(group * 2, 2)].reshape(2 * HALF, HEAD)
                h = dot_nt(keys, queries) * (0.5 * SCALE)
                grad_weights = dot_nt(values, grads)
                tanh_h = jnp.tanh(h)
                weights = h + h * tanh_h
                sigmoid_h = 0.5 + 0.5 * tanh_h
                slope = sigmoid_h + weights * (1.0 - sigmoid_h)
                visible = kcol[k_half, group] == qrow[...]
                if half == k_half:
                    inner = lax.broadcasted_iota(jnp.int32, (2 * HALF, 1), 0)
                    second = inner >= HALF
                    k_block = group * 2 + jnp.where(second, 1, 0)
                    k_in = jnp.where(second, inner - HALF, inner)
                    k_pos = (31 - k_block if half else k_block) * HALF + k_in
                    visible = visible & (k_pos <= q_pos)
                weights = jnp.where(visible, weights, 0.0).astype(BF16)
                grad_scores = jnp.where(visible, grad_weights * slope, 0.0).astype(BF16)
                dkv_acc[0, k_half, group] += dot_nn(grad_scores, queries)
                dkv_acc[1, k_half, group] += dot_nn(weights, grads)
                dq_acc[...] += dot_tn(grad_scores, keys)

            if half == 0:

                @pl.loop(low // 2, jnp.minimum(high, blocks[3]) // 2 + 1)
                def _(group):
                    step(group, 0)
            else:

                @pl.loop(low // 2, high // 2 + 1)
                def _(group):
                    step(group, 0)

                @pl.loop(jnp.maximum(low, blocks[0]) // 2, high // 2 + 1)
                def _(group):
                    step(group, 1)

            dq = (dq_acc[...] * SCALE).astype(BF16)
            for n in range(4):
                dq_ref[4 * tile + n, half] = dq[n * HALF : (n + 1) * HALF]
        return 0

    lax.fori_loop(0, 2, q_tile, 0)
    for parity in range(2):
        for half in range(2):
            rows = slice(parity * HALF, (parity + 1) * HALF)
            dkv_ref[parity, :, 0, half] = (dkv_acc[0, half, :, rows] * SCALE).astype(BF16)
            dkv_ref[parity, :, 1, half] = dkv_acc[1, half, :, rows].astype(BF16)


def attend_back(core, hist_all, q_got, kv_got, do_got):
    vmem_spec = pl.BlockSpec(memory_space=pltpu.VMEM)
    smem_spec = pl.BlockSpec(memory_space=pltpu.SMEM)
    return pl.pallas_call(
        attend_back_kernel,
        out_shape=(
            jax.ShapeDtypeStruct((8, 2, HALF, HEAD), BF16),
            jax.ShapeDtypeStruct((2, 8, 2, 2, HALF, HEAD), BF16),
        ),
        in_specs=[smem_spec, smem_spec, vmem_spec, vmem_spec, vmem_spec, vmem_spec],
        out_specs=(vmem_spec, vmem_spec),
        scratch_shapes=[
            pltpu.VMEM((2, 2, 8, ROWS, HEAD), F32),
            pltpu.VMEM((4 * HALF, HEAD), F32),
            pltpu.VMEM((2, 8, ROWS, 1), jnp.int32),
            pltpu.VMEM((1, 4 * HALF), jnp.int32),
        ],
        compiler_params=pltpu.CompilerParams(vmem_limit_bytes=VMEM_LIMIT),
        name="attend_back",
    )(core, hist_all, hist_all, q_got, kv_got, do_got)


def finish_kernel(
    dq_ref, dkv_ref, preact, w_in, grad_u, gated, tokens, grad_out, grad_tokens, out_grad,
    w_buf, pre_buf, sib_got, send_buf, got, rows_acc,
    g_send, g_got, g_sum, z_send, z_got, c_send, c_got,
    w_sem, p_sem, ssend, srecv, send_sem, recv_sem, gsend, grecv, zsend, zrecv, csend, crecv,
):
    place = Place()
    z = place.dp // 2
    my_head = place.t % HEADS

    p_copy = pltpu.make_async_copy(preact, pre_buf, p_sem)
    p_copy.start()

    def w_copy(n):
        cols = pl.ds(n * D, D)
        return pltpu.make_async_copy(w_in.at[:, cols], w_buf.at[:, cols], w_sem.at[n])

    for n in range(4):
        w_copy(n).start()

    barrier = pltpu.get_barrier_semaphore()
    for n in range(8):
        signal_if_other(place, barrier, place.worker(n))
    pl.semaphore_signal(barrier, inc=1, device_id=place.sibling)
    for n in range(1, 4):
        pl.semaphore_signal(
            barrier, inc=1, device_id={"dp": 2 * ((z + n) % 4) + place.core}
        )
    for n in range(1, CTX):
        pl.semaphore_signal(barrier, inc=1, device_id={"ctx": (place.t + n) % CTX})
    self_work = (place.t % 2 == place.core) & (place.t // HEADS == place.core)
    pl.semaphore_wait(barrier, 8 + 1 + 3 + 15 - self_work.astype(jnp.int32))

    to_sibling = pltpu.make_async_remote_copy(
        dkv_ref.at[1 - place.core], sib_got, ssend, srecv, device_id=place.sibling
    )
    to_sibling.start()

    def send_args(kind, i):
        src = dq_ref.at[i] if kind == 2 else send_buf.at[kind, i]
        return (
            place.owner(i), src, got.at[kind, my_head],
            send_sem.at[kind, i], recv_sem.at[kind, my_head],
        )

    for i in range(8):
        start_copy(place, *send_args(2, i))

    def product(chunk):
        cols = pl.ds(pl.multiple_of(chunk * 128, 128), 128)
        return dot_tn(grad_out[:, cols], gated[...])

    def to_core(n):
        return pltpu.make_async_remote_copy(
            g_send.at[n], g_got.at[n], gsend.at[n], grecv.at[n], device_id=place.sibling
        )

    for n in range(4):
        g_send[n] = product(2 * n + 1 - place.core).astype(BF16)
        to_core(n).start()

    to_sibling.wait_recv()
    for kind in range(2):
        for i in range(8):
            total = dkv_ref[place.core, i, kind].astype(F32) + sib_got[i, kind].astype(F32)
            send_buf[kind, i] = total.astype(BF16)
            start_copy(place, *send_args(kind, i))

    for n in range(4):
        g_sum[n] = product(2 * n + place.core)

    def to_plane(n):
        there = (z + n) % 4
        return pltpu.make_async_remote_copy(
            z_send.at[n - 1], z_got.at[n - 1], zsend.at[n - 1], zrecv.at[n - 1],
            device_id={"dp": 2 * there + place.core},
        )

    for n in range(4):
        to_core(n).wait_recv()
    for n in range(1, 4):
        there = (z + n) % 4
        z_send[n - 1] = (g_sum[there] + g_got[there].astype(F32)).astype(BF16)
        to_plane(n).start()

    p_copy.wait()
    w_copy(0).wait()

    def rows_part(gradient, col):
        cols = slice(col, col + D)
        _, slope = silu_and_grad(pre_buf[:, cols])
        return dot_nt((gradient * slope).astype(BF16), w_buf[:, cols])

    rows_acc[...] = rows_part(grad_u[...], U_COL)

    total = g_sum[z] + g_got[z].astype(F32)
    for n in range(1, 4):
        to_plane(n).wait_recv()
        total = total + z_got[n - 1].astype(F32)
    c_send[...] = total.reshape(CTX, 8, D)

    def to_ctx(n):
        there = (place.t + n) % CTX
        return pltpu.make_async_remote_copy(
            c_send.at[there], c_got.at[n - 1], csend.at[n - 1], crecv.at[n - 1],
            device_id={"ctx": there},
        )

    for n in range(1, CTX):
        to_ctx(n).start()

    for kind, col, w_index in ((2, Q_COL, 2), (0, K_COL, 3), (1, V_COL, 1)):
        w_copy(w_index).wait()
        for head in range(HEADS):
            wait_arrived(got.at[kind, head], recv_sem.at[kind, head])
        gradient = jnp.concatenate(
            [got[kind, head].reshape(ROWS, HEAD) for head in range(HEADS)], axis=1
        ).astype(F32)
        rows_acc[...] += rows_part(gradient, col)

    normed, inv_x = norm_rows(tokens[...].astype(F32))
    grad_tokens[...] = (
        grad_out[...].astype(F32) + norm_back(rows_acc[...], normed, inv_x)
    ).astype(BF16)

    total = c_send[place.t]
    for n in range(1, CTX):
        to_ctx(n).wait_recv()
        total = total + c_got[n - 1]
    out_grad[...] = total * (24576.0 ** (-0.5))

    to_sibling.wait_send()
    for n in range(4):
        to_core(n).wait_send()
    for n in range(1, 4):
        to_plane(n).wait_send()
    for n in range(1, CTX):
        to_ctx(n).wait_send()
    for i in range(8):
        for kind in range(3):
            wait_sent(place, *send_args(kind, i))


def finish(dq, dkv, preact, w_in, grad_u, gated, tokens, grad_out):
    any_spec = pl.BlockSpec(memory_space=pl.ANY)
    vmem_spec = pl.BlockSpec(memory_space=pltpu.VMEM)
    dma = pltpu.SemaphoreType.DMA
    return pl.pallas_call(
        finish_kernel,
        out_shape=(
            jax.ShapeDtypeStruct((ROWS, D), BF16),
            jax.ShapeDtypeStruct((8, D), F32),
        ),
        in_specs=[vmem_spec, vmem_spec, any_spec, any_spec] + [vmem_spec] * 4,
        out_specs=(vmem_spec, vmem_spec),
        scratch_shapes=[
            pltpu.VMEM((D, 4 * D), BF16),
            pltpu.VMEM((ROWS, 4 * D), F32),
            pltpu.VMEM((8, 2, 2, HALF, HEAD), BF16),
            pltpu.VMEM((2, 8, 2, HALF, HEAD), BF16),
            pltpu.VMEM((3, HEADS, 2, HALF, HEAD), BF16),
            pltpu.VMEM((ROWS, D), F32),
            pltpu.VMEM((4, 128, D), BF16),
            pltpu.VMEM((4, 128, D), BF16),
            pltpu.VMEM((4, 128, D), F32),
            pltpu.VMEM((3, 128, D), BF16),
            pltpu.VMEM((3, 128, D), BF16),
            pltpu.VMEM((CTX, 8, D), F32),
            pltpu.VMEM((CTX - 1, 8, D), F32),
            dma((4,)), dma, dma, dma, dma((3, 8)), dma((3, 8)),
            dma((4,)), dma((4,)), dma((3,)), dma((3,)), dma((CTX - 1,)), dma((CTX - 1,)),
        ],
        compiler_params=pltpu.CompilerParams(
            collective_id=2, has_side_effects=True, vmem_limit_bytes=VMEM_LIMIT
        ),
        name="return_and_finish",
    )(dq, dkv, preact, w_in, grad_u, gated, tokens, grad_out)


def on_device(tokens, segments, w_in, w_out, grad_out):
    core = (lax.axis_index("dp") % 2).astype(jnp.int32).reshape(1)
    q_got, kv_got, hist_all, u_act, preact = project(tokens, segments, w_in)
    o_loc = attend(core, hist_all, q_got, kv_got)
    layer_out, do_got, gated, grad_u = middle(o_loc, tokens, u_act, grad_out, w_out)
    dq, dkv = attend_back(core, hist_all, q_got, kv_got, do_got)
    grad_tokens, out_grad = finish(dq, dkv, preact, w_in, grad_u, gated, tokens, grad_out)
    return (layer_out, grad_tokens, out_grad)


def solution(mesh):
    return jax.shard_map(
        on_device,
        mesh=mesh,
        in_specs=(P(("dp", "ctx"), None), P("dp", "ctx"), P(), P(), P(("dp", "ctx"), None)),
        out_specs=(P(("dp", "ctx"), None), P(("dp", "ctx"), None), P(("dp", "ctx"), None)),
        check_vma=False,
    )
```

time: 1010 us -> 125 us (0.12)
  waiting for transfers between devices: 703 us -> 0 us
  matrix products: 167 us -> 0 us
  Pallas kernels: 0 us -> 120 us
  blocking collectives: 62.2 us -> 0 us
  local copies, waits for them, and re-layouts: 49.4 us -> 3.89 us
  between operations: 14.7 us -> 0.68 us
    unnamed x6 -> x0, waiting for transfers between devices: 561 us -> none
    dot_general x53 -> x0, matrix products: 167 us -> none  [the longest x8 34.5 us: query_head(): return jnp.dot(grad_scores, one_k, preferred_element_type=jnp.float32)]
    all_gather x4 -> x0, waiting for transfers between devices: 143 us -> none  [the longest x1 87.1 us: on_device(): piece_grad = lax.all_gather(grad_mixed, 'ctx', axis=0, tiled=True)]
    pallas_call x0 -> x5, Pallas kernels: none -> 120 us  [the longest x1 34.1 us: finish(): pl.pallas_call(finish_kernel, out_shape=(jax.ShapeDtypeStruct((ROWS, D),...]
    all_gather x1 -> x0, blocking collectives: 62.2 us -> none  [on_device(): lax.all_gather(history, 'ctx', axis=0, tiled=True)]
    transpose x6 -> x0, local copies, waits for them, and re-layouts: 30.2 us -> none  [head_major(): matrix.reshape(matrix.shape[0], HEADS, matrix.shape[1] // HEADS)]
  transfers between devices with their start and end apart: 5 -> 0, of which waited for: 3 -> 0; matrix products, arithmetic and copies ran while one was open for 13% -> 0% of each run, Pallas kernels for 0% -> 0%
where the time goes in v1:
time: 125 us; the launch traced here: 124 us
  Pallas kernels  120 us (96%)
  local copies, waits for them, and re-layouts  3.89 us (3%)
    pallas_call x1, Pallas kernels, finish(): pl.pallas_call(finish_kernel, out_shape=(jax.ShapeDtypeStruct((ROWS, D),...  34.1 us
    pallas_call x1, Pallas kernels, project(): pl.pallas_call(project_kernel, out_shape=(jax.ShapeDtypeStruct((8, 2, HAL...  24.8 us
    pallas_call x1, Pallas kernels, attend_back(): pl.pallas_call(attend_back_kernel, out_shape=(jax.ShapeDtypeStruct((8, 2,...  24.5 us
    pallas_call x1, Pallas kernels, middle(): pl.pallas_call(middle_kernel, out_shape=(jax.ShapeDtypeStruct((ROWS, D),...  21.9 us
    pallas_call x1, Pallas kernels, attend(): pl.pallas_call(attend_kernel, out_shape=jax.ShapeDtypeStruct((8, 2, HALF,...  14.6 us
    unnamed x5, local copies, waits for them, and re-layouts  3.89 us

profile of v1, /device:TPU:1, one launch (start us, length us, event | category | flops | bytes accessed | tf_op | source)
XLA Modules:
  0.0 124.5 jit_solution(183017558094892167)
XLA Ops:
  0.6 24.8 %project_and_send.1 = (bf16[8,2,96,128]{3,2,1,0:T(8,128)(2,1)}, bf16[2,2,16,96,128]{4,3,2,1,0:T(8,128)(2,1)}, s32[16,1,256]{2,1,0:T(1,128)}, bf16[192,1024]{1,0:T(8,128)(2,1)}, f32[192,4096]{1,0:T(8,128)}) custom-call(bf16[192,1024]{1,0:T(8,128)(2,1)} %tokens.5, s32[1,192]{1,0:T(1,128)} %hist.1, bf16[1024,4096]{1,0:T(8,128)(2,1)} %w_in.3), custom_call_target="tpu_custom_call" | custom-call | tf_op jit(solution)/shard_map/project_and_send/pallas_call | solution.py:223
  25.5 14.6 %attend.1.o_ref = bf16[8,2,96,128]{3,2,1,0:T(8,128)(2,1)} custom-call(s32[1]{0:T(128)} %bitcast.core_s, s32[16,1,256]{2,1,0:T(1,128)} %get-tuple-element.16.hist_s.hist_v, s32[16,1,256]{2,1,0:T(1,128)} %get-tuple-element.16.hist_s.hist_v, bf16[8,2,96,128]{3,2,1,0:T(8,128)(2,1)} %get-tuple-element.17.q_ref, bf16[2,2,16,96,128]{4,3,2,1,0:T(8,128)(2,1)} %get-tuple-element.18.kv_ref), custom_call_target="tpu_custom_call" | custom-call | tf_op jit(solution)/shard_map/attend/pallas_call | solution.py:337
  40.1 21.9 %gate_and_send.1 = (bf16[192,1024]{1,0:T(8,128)(2,1)}, bf16[8,2,96,128]{3,2,1,0:T(8,128)(2,1)}, bf16[192,1024]{1,0:T(8,128)(2,1)}, f32[192,1024]{1,0:T(8,128)}) custom-call(bf16[8,2,96,128]{3,2,1,0:T(8,128)(2,1)} %attend.1.o_ref, bf16[192,1024]{1,0:T(8,128)(2,1)} %tokens.5, bf16[192,1024]{1,0:T(8,128)(2,1)} %get-tuple-element.19.u_act, ...), custom_call_target="tpu_custom_call" | custom-call | tf_op jit(solution)/shard_map/gate_and_send/pallas_call | solution.py:407
  62.0 24.5 %attend_back.1 = (bf16[8,2,96,128]{3,2,1,0:T(8,128)(2,1)}, bf16[2,8,2,2,96,128]{5,4,3,2,1,0:T(8,128)(2,1)}) custom-call(s32[1]{0:T(128)} %bitcast.core_s, s32[16,1,256]{2,1,0:T(1,128)} %get-tuple-element.16.hist_s.hist_v, s32[16,1,256]{2,1,0:T(1,128)} %get-tuple-element.16.hist_s.hist_v, bf16[8,2,96,128]{3,2,1,0:T(8,128)(2,1)} %get-tuple-element.17.q_ref, ...), custom_call_target="tpu_custom_call" | custom-call | tf_op jit(solution)/shard_map/attend_back/pallas_call | solution.py:510
  86.5 0.0 copy-start
  86.5 34.1 %return_and_finish.1 = (bf16[192,1024]{1,0:T(8,128)(2,1)}, f32[8,1024]{1,0:T(8,128)}) custom-call(bf16[8,2,96,128]{3,2,1,0:T(8,128)(2,1)} %get-tuple-element.22.dq_ref, bf16[2,8,2,2,96,128]{5,4,3,2,1,0:T(8,128)(2,1)} %get-tuple-element.23.dkv_ref, f32[192,4096]{1,0:T(8,128)} %get-tuple-element.24.preact, bf16[1024,4096]{1,0:T(8,128)(2,1)} %w_in.3, ...), custom_call_target="tpu_custom_call" | custom-call | tf_op jit(solution)/shard_map/return_and_finish/pallas_call | solution.py:676
  120.6 0.0 copy-done
  120.6 0.7 copy.11
  121.3 1.8 %copy.12 = bf16[192,1024]{1,0:T(8,128)(2,1)} copy(bf16[192,1024]{1,0:T(8,128)(2,1)} %get-tuple-element.33) | data formatting | bytes 786432
  123.1 1.4 %copy.13 = f32[8,1024]{1,0:T(8,128)} copy(f32[8,1024]{1,0:T(8,128)} %get-tuple-element.34) | data formatting | bytes 65536
Async XLA Ops:
  86.5 34.1 %copy-start = (bf16[192,1024]{1,0:T(8,128)(2,1)S(1)}, bf16[192,1024]{1,0:T(8,128)(2,1)}, u32[]{:S(2)}) copy-start(bf16[192,1024]{1,0:T(8,128)(2,1)} %get-tuple-element.32) | copy-start | bytes 1179652

commit v2 on v0

v2 whole, which is shorter than its diff:
```python
import jax
import jax.numpy as jnp
from jax import lax
from jax.experimental import pallas as pl
from jax.experimental.pallas import tpu as pltpu
from jax.sharding import PartitionSpec as P

HEADS = 8
HEAD = 128
ROWS = 192
HALF = 96
D = 1024
CTX = 16
G = 4 * HALF
EPS = 1e-05
SCALE = HEAD ** (-0.5)
VMEM_LIMIT = 60 * 1024 * 1024
F32 = jnp.float32
BF16 = jnp.bfloat16
U_COL, V_COL, Q_COL, K_COL = 0, D, 2 * D, 3 * D
KEY, QUERY, VALUE, GNORM = 0, 1, 2, 3

TILES = [(0, 0, 0, 0), (0, 0, 0, 1)]
TILES += [(1, 0, 0, g) for g in range(4)] + [(1, 0, 1, g) for g in range(4)]
TILES += [(0, 1, 0, g) for g in range(4)]
TILES += [(1, 1, 0, g) for g in range(4)] + [(1, 1, 1, g) for g in (2, 3)]


def norm_rows(matrix):
    average = jnp.mean(matrix, axis=-1, keepdims=True)
    centred = matrix - average
    inverse = lax.rsqrt(jnp.mean(centred * centred, axis=-1, keepdims=True) + EPS)
    return centred * inverse, inverse


def norm_back(gradient, normed, inverse):
    first = jnp.mean(gradient, axis=-1, keepdims=True)
    second = jnp.mean(gradient * normed, axis=-1, keepdims=True)
    return (gradient - first - normed * second) * inverse


def dot_nt(left, right):
    return lax.dot_general(left, right, (((1,), (1,)), ((), ())), preferred_element_type=F32)


def dot_tn(left, right):
    return lax.dot_general(left, right, (((0,), (0,)), ((), ())), preferred_element_type=F32)


def dot_nn(left, right):
    return lax.dot_general(left, right, (((1,), (0,)), ((), ())), preferred_element_type=F32)


def flat(blocks):
    return blocks.reshape(-1, HEAD)


class Place:
    def __init__(self):
        self.dp = lax.axis_index("dp")
        self.t = lax.axis_index("ctx")
        self.plane = 2 * (self.dp // 2)
        self.core = self.dp % 2
        self.z = self.dp // 2
        self.sibling = {"dp": self.plane + 1 - self.core}
        self.head = self.t % HEADS
        self.slot = self.t // 2

    def worker(self, head):
        return self.plane + self.t % 2, self.core * HEADS + head

    def owner(self, i):
        return self.plane + self.t // HEADS, 2 * i + self.core

    def is_me(self, device):
        return (device[0] == self.dp) & (device[1] == self.t)

    def has_self(self):
        return (self.t % 2 == self.core) & (self.t // HEADS == self.core)


def ident(device):
    return {"dp": device[0], "ctx": device[1]}


def signal_if_other(place, barrier, device):
    @pl.when(jnp.logical_not(place.is_me(device)))
    def _():
        pl.semaphore_signal(barrier, inc=1, device_id=ident(device))


def start_copy(place, device, src, dst, send_sem, recv_sem):
    mine = place.is_me(device)

    @pl.when(mine)
    def _():
        pltpu.make_async_copy(src, dst, recv_sem).start()

    @pl.when(jnp.logical_not(mine))
    def _():
        pltpu.make_async_remote_copy(
            src, dst, send_sem, recv_sem, device_id=ident(device)
        ).start()


def wait_sent(place, device, src, dst, send_sem, recv_sem):
    @pl.when(jnp.logical_not(place.is_me(device)))
    def _():
        pltpu.make_async_remote_copy(
            src, dst, send_sem, recv_sem, device_id=ident(device)
        ).wait_send()


def wait_arrived(dst, recv_sem):
    pltpu.make_async_copy(dst, dst, recv_sem).wait()


def history_masks(hist_all, khist, qhist, core):
    for half in range(2):
        lanes = slice(half * 128, half * 128 + HALF)
        for g in range(4):
            row = jnp.concatenate([hist_all[4 * g + n, :, lanes] for n in range(4)], axis=1)
            rows = jnp.broadcast_to(row.astype(F32).astype(BF16), (16, G))
            khist[half, g] = dot_tn(rows, jnp.full((16, 128), 1.0 / 16, BF16))
        for g in range(2):
            row = jnp.concatenate(
                [hist_all[8 * g + 2 * n + core, :, lanes] for n in range(4)], axis=1
            )
            qhist[half, g] = row.astype(F32)


def query_positions(half, g, core):
    lane = lax.broadcasted_iota(jnp.int32, (1, G), 1)
    inside = lane // HALF
    block = 8 * g + 2 * inside + core
    return (31 - block if half else block) * HALF + lane - inside * HALF


def key_positions(half, g):
    row = lax.broadcasted_iota(jnp.int32, (G, 128), 0)
    inside = row // HALF
    block = 4 * g + inside
    return (31 - block if half else block) * HALF + row - inside * HALF


def three(matrix):
    return jnp.concatenate([matrix, matrix, matrix], axis=1)


def score_tile(n, q_got, k_got, khist, qhist, p_buf, s_buf, core):
    qh, qg, kh, kg = TILES[n]
    half = dot_nt(
        flat(k_got[kh, 4 * kg : 4 * kg + 4]), flat(q_got[qh, 4 * qg : 4 * qg + 4])
    ) * (0.5 * SCALE)
    up = 1.0 + jnp.tanh(half)
    weights = half * up
    slope = weights + (0.5 * up) * (1.0 - weights)
    visible = three(khist[kh, kg]) == qhist[qh, qg]
    if qh == kh and kg // 2 == qg:
        visible = visible & (three(key_positions(kh, kg)) <= query_positions(qh, qg, core))
    p_buf[n] = jnp.where(visible, weights, 0.0).astype(BF16)
    s_buf[n] = jnp.where(visible, slope, 0.0).astype(BF16)


def mix_tiles(qh, qg, vt, p_buf):
    total = None
    for n, tile in enumerate(TILES):
        if tile[:2] == (qh, qg):
            part = dot_nn(vt[tile[2], tile[3]], p_buf[n])
            total = part if total is None else total + part
    return total


def back_keys(kh, kg, q_got, v_got, kt, dot_buf, p_buf, s_buf, dqt):
    values = flat(v_got[kh, 4 * kg : 4 * kg + 4])
    grad_k = grad_v = None
    for n, tile in enumerate(TILES):
        if tile[2:] != (kh, kg):
            continue
        qh, qg = tile[:2]
        grads = dot_buf[qh, qg]
        grad_scores = (dot_nn(values, grads) * s_buf[n].astype(F32)).astype(BF16)
        part_v = dot_nt(p_buf[n], grads)
        part_k = dot_nn(grad_scores, flat(q_got[qh, 4 * qg : 4 * qg + 4]))
        grad_v = part_v if grad_v is None else grad_v + part_v
        grad_k = part_k if grad_k is None else grad_k + part_k
        dqt[qh, qg] += dot_nn(kt[kh, kg], grad_scores)
    return grad_k, grad_v


def layer_kernel(
    tokens_in, hist, w_in, w_out_in, grad_out_in,
    layer_out, grad_tokens, out_grad,
    tokens, grad_out, w_buf, w_out, normed_buf, slope_buf, u_buf, gate_buf,
    hist_buf, hist_all, khist, qhist,
    send_buf, k_got, v_got, q_got, n_got,
    p_buf, s_buf, vt, kt, ot_buf, gt_buf, o_send, mixed_got, stats, dot_buf, dqt,
    part, part_send, sib_got, ret_send, ret_got, rows_acc,
    go_sib, gated_buf, gated_sib, g_sum, z_send, z_got, c_send, c_got,
    in_sem, w_sem, hsend, hrecv, hfsend, hfrecv, send_sem, recv_sem, fsend, frecv,
    osend, orecv, ssend, srecv, psend, precv, rsend, rrecv,
    gosend, gorecv, gdsend, gdrecv, zsend, zrecv, csend, crecv,
):
    place = Place()
    core, t, z, my_head, slot = place.core, place.t, place.z, place.head, place.slot

    t_copy = pltpu.make_async_copy(tokens_in, tokens, in_sem.at[0])
    t_copy.start()
    chunks = [K_COL, K_COL + 512, Q_COL, Q_COL + 512, V_COL, V_COL + 512, U_COL, U_COL + 512]

    def w_copy(n):
        cols = pl.ds(chunks[n], 512)
        return pltpu.make_async_copy(w_in.at[:, cols], w_buf.at[:, cols], w_sem.at[n])

    for n in range(2):
        w_copy(n).start()
    go_copy = pltpu.make_async_copy(grad_out_in, grad_out, in_sem.at[1])
    go_copy.start()
    for n in range(2, 8):
        w_copy(n).start()
    wo_copy = pltpu.make_async_copy(w_out_in, w_out, in_sem.at[2])
    wo_copy.start()

    barrier = pltpu.get_barrier_semaphore()
    for n in range(8):
        signal_if_other(place, barrier, place.owner(n))
        signal_if_other(place, barrier, place.worker(n))
    pl.semaphore_signal(barrier, inc=1, device_id=place.sibling)
    for n in range(1, 4):
        pl.semaphore_signal(barrier, inc=1, device_id={"dp": 2 * ((z + n) % 4) + core})
    for n in range(1, CTX):
        pl.semaphore_signal(barrier, inc=1, device_id={"ctx": (t + n) % CTX})

    hist_buf[...] = jnp.zeros_like(hist_buf)
    hist_buf[:, 0:HALF] = hist[:, 0:HALF]
    hist_buf[:, 128 : 128 + HALF] = hist[:, HALF:ROWS]
    t_copy.wait()
    normed_buf[...] = norm_rows(tokens[...].astype(F32))[0].astype(BF16)

    def send_args(kind, head):
        got = (k_got, q_got, v_got, n_got)[kind]
        dst = got.at[:, t] if kind in (KEY, VALUE) else got.at[:, slot]
        return (
            place.worker(head), send_buf.at[kind, head], dst,
            send_sem.at[kind, head], recv_sem.at[kind, slot],
        )

    def hist_args(head):
        return place.worker(head), hist_buf, hist_all.at[t], hsend.at[head], hrecv.at[slot]

    def go_to_sibling(n):
        cols = pl.ds(pl.multiple_of((2 * n + 1 - core) * 128, 128), 128)
        return pltpu.make_async_remote_copy(
            grad_out.at[:, cols], go_sib.at[n], gosend.at[n], gorecv.at[n],
            device_id=place.sibling,
        )

    def project(n):
        w_copy(n).wait()
        cols = slice(chunks[n], chunks[n] + 512)
        half = 0.5 * dot_nn(normed_buf[...], w_buf[:, cols])
        up = 1.0 + jnp.tanh(half)
        act = half * up
        slope_buf[:, cols] = act + (0.5 * up) * (1.0 - act)
        return act.astype(BF16)

    for n in range(8):
        act = project(n)
        if n == 0:
            pl.semaphore_wait(barrier, 16 + 1 + 3 + 15 - 2 * place.has_self().astype(jnp.int32))
            for head in range(HEADS):
                start_copy(place, *hist_args(head))
        if n < 6:
            for j in range(4):
                head = (n % 2) * 4 + j
                send_buf[n // 2, head] = act[:, j * 128 : (j + 1) * 128].reshape(2, HALF, HEAD)
                start_copy(place, *send_args(n // 2, head))
        else:
            u_buf[:, chunks[n] : chunks[n] + 512] = act

    go_copy.wait()
    for n in range(4):
        go_to_sibling(n).start()
    wo_copy.wait()
    gate_buf[...] = dot_nt(grad_out[...], w_out[...])
    grad_norm = (gate_buf[...] * u_buf[...].astype(F32)).astype(BF16)
    for head in range(HEADS):
        send_buf[GNORM, head] = grad_norm[:, head * 128 : (head + 1) * 128].reshape(2, HALF, HEAD)
        start_copy(place, *send_args(GNORM, head))

    def hist_forward(i):
        c = 2 * i + core
        return pltpu.make_async_remote_copy(
            hist_all.at[c], hist_all.at[c], hfsend.at[i], hfrecv.at[i], device_id=place.sibling
        )

    def forward(kind, i):
        ref = (k_got, None, v_got)[kind].at[:, 2 * i + core]
        return pltpu.make_async_remote_copy(
            ref, ref, fsend.at[kind // 2, i], frecv.at[kind // 2, i], device_id=place.sibling
        )

    def pass_on(kind):
        got = (k_got, None, v_got)[kind]
        for i in range(8):
            wait_arrived(got.at[:, 2 * i + core], recv_sem.at[kind, i])
            forward(kind, i).start()

    def wait_passed(kind):
        got = (k_got, None, v_got)[kind]
        for i in range(8):
            wait_arrived(got.at[:, 2 * i + 1 - core], frecv.at[kind // 2, i])

    for i in range(8):
        wait_arrived(hist_all.at[2 * i + core], hrecv.at[i])
        hist_forward(i).start()
    for i in range(8):
        wait_arrived(hist_all.at[2 * i + 1 - core], hfrecv.at[i])
    history_masks(hist_all, khist, qhist, core)

    pass_on(KEY)
    for i in range(8):
        wait_arrived(q_got.at[:, i], recv_sem.at[QUERY, i])
    wait_passed(KEY)
    for n in range(12):
        score_tile(n, q_got, k_got, khist, qhist, p_buf, s_buf, core)
    pass_on(VALUE)
    for n in range(12, len(TILES)):
        score_tile(n, q_got, k_got, khist, qhist, p_buf, s_buf, core)
    wait_passed(VALUE)
    for half in range(2):
        for g in range(4):
            vt[half, g] = flat(v_got[half, 4 * g : 4 * g + 4]).T

    def o_args(i):
        return (
            place.owner(i), o_send.at[:, i], mixed_got.at[my_head], osend.at[i], orecv.at[my_head],
        )

    for qg in range(2):
        for qh in range(2):
            mixed_t = mix_tiles(qh, qg, vt, p_buf)
            ot_buf[qh, qg] = mixed_t
            o_send[qh, 4 * qg : 4 * qg + 4] = mixed_t.T.astype(BF16).reshape(4, HALF, HEAD)
            average = jnp.mean(mixed_t, axis=0, keepdims=True)
            centred = mixed_t - average
            stats[my_head, qg, 4 * qh : 4 * qh + 1] = average
            stats[my_head, qg, 4 * qh + 1 : 4 * qh + 2] = jnp.sum(
                centred * centred, axis=0, keepdims=True
            )
        for i in range(4 * qg, 4 * qg + 4):
            start_copy(place, *o_args(i))

    def stats_copy(n):
        there = (t // HEADS) * HEADS + (my_head + n) % HEADS
        return pltpu.make_async_remote_copy(
            stats.at[my_head], stats.at[my_head], ssend.at[n - 1], srecv.at[n - 1],
            device_id={"ctx": there},
        )

    for i in range(8):
        wait_arrived(n_got.at[:, i], recv_sem.at[GNORM, i])
    for qg in range(2):
        for qh in range(2):
            grad_t = flat(n_got[qh, 4 * qg : 4 * qg + 4]).T
            gt_buf[qh, qg] = grad_t
            grad_t = grad_t.astype(F32)
            average = stats[my_head, qg, 4 * qh : 4 * qh + 1]
            stats[my_head, qg, 4 * qh + 2 : 4 * qh + 3] = jnp.sum(grad_t, axis=0, keepdims=True)
            stats[my_head, qg, 4 * qh + 3 : 4 * qh + 4] = jnp.sum(
                grad_t * (ot_buf[qh, qg] - average), axis=0, keepdims=True
            )
    for n in range(1, HEADS):
        stats_copy(n).start()
    for half in range(2):
        for g in range(4):
            kt[half, g] = flat(k_got[half, 4 * g : 4 * g + 4]).T
    dqt[...] = jnp.zeros_like(dqt)
    for n in range(1, HEADS):
        wait_arrived(stats.at[(my_head + HEADS - n) % HEADS], srecv.at[n - 1])
    for qg in range(2):
        for qh in range(2):
            rows = [[stats[h, qg, 4 * qh + k : 4 * qh + k + 1] for h in range(HEADS)] for k in range(4)]
            average = sum(rows[0]) * (1.0 / HEADS)
            off = [row - average for row in rows[0]]
            spread = sum(rows[1]) + HEAD * sum(o * o for o in off)
            inverse = lax.rsqrt(spread * (1.0 / D) + EPS)
            first = sum(rows[2]) * (1.0 / D)
            second = (sum(rows[3]) + sum(o * a for o, a in zip(off, rows[2]))) * (1.0 / D)
            centred = ot_buf[qh, qg] - average
            dot_buf[qh, qg] = (
                (gt_buf[qh, qg].astype(F32) - first - centred * (second * inverse * inverse))
                * inverse
            ).astype(BF16)

    def gate():
        for head in range(HEADS):
            wait_arrived(mixed_got.at[head], orecv.at[head])
        mixed = jnp.concatenate([flat(mixed_got[head]) for head in range(HEADS)], axis=1)
        mixed_n, _ = norm_rows(mixed.astype(F32))
        gated = (mixed_n * u_buf[...].astype(F32)).astype(BF16)
        gated_buf[...] = gated
        gated_copy.start()
        grad_pre = (gate_buf[...] * mixed_n * slope_buf[:, U_COL : U_COL + D]).astype(BF16)
        layer_out[...] = (dot_nn(gated, w_out[...]) + tokens[...].astype(F32)).astype(BF16)
        rows_acc[...] = dot_nt(grad_pre, w_buf[:, U_COL : U_COL + D])

    gated_copy = pltpu.make_async_remote_copy(
        gated_buf, gated_sib, gdsend, gdrecv, device_id=place.sibling
    )

    def to_plane(n):
        return pltpu.make_async_remote_copy(
            z_send.at[n - 1], z_got.at[n - 1], zsend.at[n - 1], zrecv.at[n - 1],
            device_id={"dp": 2 * ((z + n) % 4) + core},
        )

    def products():
        gated_copy.wait_recv()
        for n in range(4):
            go_to_sibling(n).wait_recv()
        for n in (2, 1, 3, 0):
            there = (z + n) % 4
            cols = pl.ds(pl.multiple_of((2 * there + core) * 128, 128), 128)
            product = dot_tn(grad_out[:, cols], gated_buf[...]) + dot_tn(
                go_sib[there], gated_sib[...]
            )
            if n:
                z_send[n - 1] = product.astype(BF16)
                to_plane(n).start()
            else:
                g_sum[...] = product

    def part_copy(kind, kg, kh):
        ref = part_send.at[kind, kg, kh]
        return pltpu.make_async_remote_copy(
            ref, sib_got.at[kind, kg, kh], psend.at[kind, kg, kh], precv.at[kind, kg, kh],
            device_id=place.sibling,
        )

    def ret_args(kind, i):
        return (
            place.owner(i), ret_send.at[kind, i], ret_got.at[kind, my_head],
            rsend.at[kind, i], rrecv.at[kind, my_head],
        )

    def back_group(kg):
        for kh in range(2):
            grads = back_keys(kh, kg, q_got, v_got, kt, dot_buf, p_buf, s_buf, dqt)
            for kind in range(2):
                grad = grads[kind] * SCALE if kind == 0 else grads[kind]
                grad = grad.reshape(2, 2, HALF, HEAD)
                for parity in range(2):
                    part[kind, kg, kh, parity] = grad[:, parity]
                part_send[kind, kg, kh] = part[kind, kg, kh, 1 - core].astype(BF16)
                part_copy(kind, kg, kh).start()

    def return_group(kg):
        for kind in (1, 0):
            for kh in range(2):
                part_copy(kind, kg, kh).wait_recv()
                total = part[kind, kg, kh, core] + sib_got[kind, kg, kh].astype(F32)
                for n in range(2):
                    ret_send[kind, 2 * kg + n, kh] = total[n].astype(BF16)
            for n in range(2):
                start_copy(place, *ret_args(kind, 2 * kg + n))

    back_group(0)
    gate()
    back_group(1)
    return_group(0)
    products()
    back_group(2)
    return_group(1)
    back_group(3)
    return_group(2)
    for qg in range(2):
        for qh in range(2):
            grad_q = (dqt[qh, qg] * SCALE).T.astype(BF16).reshape(4, HALF, HEAD)
            for n in range(4):
                ret_send[2, 4 * qg + n, qh] = grad_q[n]
        if qg == 0:
            return_group(3)
        for i in range(4 * qg, 4 * qg + 4):
            start_copy(place, *ret_args(2, i))

    total = g_sum[...]
    for n in range(1, 4):
        to_plane(n).wait_recv()
        total = total + z_got[n - 1].astype(F32)
    c_send[...] = total.reshape(CTX, 8, D)

    def to_ctx(n):
        there = (t + n) % CTX
        return pltpu.make_async_remote_copy(
            c_send.at[there], c_got.at[n - 1], csend.at[n - 1], crecv.at[n - 1],
            device_id={"ctx": there},
        )

    for n in range(1, CTX):
        to_ctx(n).start()

    for kind, col in ((1, V_COL), (0, K_COL), (2, Q_COL)):
        for head in range(HEADS):
            wait_arrived(ret_got.at[kind, head], rrecv.at[kind, head])
        gradient = jnp.concatenate([flat(ret_got[kind, head]) for head in range(HEADS)], axis=1)
        grad_pre = (gradient.astype(F32) * slope_buf[:, col : col + D]).astype(BF16)
        rows_acc[...] += dot_nt(grad_pre, w_buf[:, col : col + D])

    normed, inv_x = norm_rows(tokens[...].astype(F32))
    grad_tokens[...] = (
        grad_out[...].astype(F32) + norm_back(rows_acc[...], normed, inv_x)
    ).astype(BF16)

    total = c_send[t]
    for n in range(1, CTX):
        to_ctx(n).wait_recv()
        total = total + c_got[n - 1]
    out_grad[...] = total * (24576.0 ** (-0.5))

    for n in range(4):
        go_to_sibling(n).wait_send()
    gated_copy.wait_send()
    for n in range(1, 4):
        to_plane(n).wait_send()
    for n in range(1, CTX):
        to_ctx(n).wait_send()
    for n in range(1, HEADS):
        stats_copy(n).wait_send()
    for i in range(8):
        hist_forward(i).wait_send()
        forward(KEY, i).wait_send()
        forward(VALUE, i).wait_send()
        wait_sent(place, *hist_args(i))
        for kind in range(4):
            wait_sent(place, *send_args(kind, i))
        wait_sent(place, *o_args(i))
        for kind in range(3):
            wait_sent(place, *ret_args(kind, i))
    for kind in range(2):
        for kg in range(4):
            for kh in range(2):
                part_copy(kind, kg, kh).wait_send()


def on_device(tokens, segments, w_in, w_out, grad_out):
    any_spec = pl.BlockSpec(memory_space=pl.ANY)
    vmem_spec = pl.BlockSpec(memory_space=pltpu.VMEM)
    dma = pltpu.SemaphoreType.DMA
    vmem = pltpu.VMEM
    tiles = len(TILES)
    return pl.pallas_call(
        layer_kernel,
        out_shape=(
            jax.ShapeDtypeStruct((ROWS, D), BF16),
            jax.ShapeDtypeStruct((ROWS, D), BF16),
            jax.ShapeDtypeStruct((8, D), F32),
        ),
        in_specs=[any_spec, vmem_spec, any_spec, any_spec, any_spec],
        out_specs=(vmem_spec, vmem_spec, vmem_spec),
        scratch_shapes=[
            vmem((ROWS, D), BF16),
            vmem((ROWS, D), BF16),
            vmem((D, 4 * D), BF16),
            vmem((D, D), BF16),
            vmem((ROWS, D), BF16),
            vmem((ROWS, 4 * D), F32),
            vmem((ROWS, D), BF16),
            vmem((ROWS, D), F32),
            vmem((1, 256), jnp.int32),
            vmem((CTX, 1, 256), jnp.int32),
            vmem((2, 4, G, 128), F32),
            vmem((2, 2, 1, G), F32),
            vmem((4, HEADS, 2, HALF, HEAD), BF16),
            vmem((2, CTX, HALF, HEAD), BF16),
            vmem((2, CTX, HALF, HEAD), BF16),
            vmem((2, 8, HALF, HEAD), BF16),
            vmem((2, 8, HALF, HEAD), BF16),
            vmem((tiles, G, G), BF16),
            vmem((tiles, G, G), BF16),
            vmem((2, 4, HEAD, G), BF16),
            vmem((2, 4, HEAD, G), BF16),
            vmem((2, 2, HEAD, G), F32),
            vmem((2, 2, HEAD, G), BF16),
            vmem((2, 8, HALF, HEAD), BF16),
            vmem((HEADS, 2, HALF, HEAD), BF16),
            vmem((HEADS, 2, 8, G), F32),
            vmem((2, 2, HEAD, G), BF16),
            vmem((2, 2, HEAD, G), F32),
            vmem((2, 4, 2, 2, 2, HALF, HEAD), F32),
            vmem((2, 4, 2, 2, HALF, HEAD), BF16),
            vmem((2, 4, 2, 2, HALF, HEAD), BF16),
            vmem((3, 8, 2, HALF, HEAD), BF16),
            vmem((3, HEADS, 2, HALF, HEAD), BF16),
            vmem((ROWS, D), F32),
            vmem((4, ROWS, 128), BF16),
            vmem((ROWS, D), BF16),
            vmem((ROWS, D), BF16),
            vmem((128, D), F32),
            vmem((3, 128, D), BF16),
            vmem((3, 128, D), BF16),
            vmem((CTX, 8, D), F32),
            vmem((CTX - 1, 8, D), F32),
            dma((3,)), dma((8,)),
            dma((8,)), dma((8,)), dma((8,)), dma((8,)),
            dma((4, 8)), dma((4, 8)), dma((2, 8)), dma((2, 8)),
            dma((8,)), dma((8,)), dma((HEADS - 1,)), dma((HEADS - 1,)),
            dma((2, 4, 2)), dma((2, 4, 2)), dma((3, 8)), dma((3, 8)),
            dma((4,)), dma((4,)), dma, dma,
            dma((3,)), dma((3,)), dma((CTX - 1,)), dma((CTX - 1,)),
        ],
        compiler_params=pltpu.CompilerParams(
            collective_id=0, has_side_effects=True, vmem_limit_bytes=VMEM_LIMIT
        ),
        name="layer",
    )(tokens, segments, w_in, w_out, grad_out)


def solution(mesh):
    return jax.shard_map(
        on_device,
        mesh=mesh,
        in_specs=(P(("dp", "ctx"), None), P("dp", "ctx"), P(), P(), P(("dp", "ctx"), None)),
        out_specs=(P(("dp", "ctx"), None), P(("dp", "ctx"), None), P(("dp", "ctx"), None)),
        check_vma=False,
    )
```

time: 1010 us -> 79.9 us (0.08)
  the two profiles are of different devices: /device:TPU:1 before, /device:TPU:24 now
where the time goes in v2:
time: 79.9 us; the launch traced here: 79.6 us
  Pallas kernels  74 us (93%)
  local copies, waits for them, and re-layouts  4.91 us (6%)
    pallas_call x1, Pallas kernels, on_device(): pl.pallas_call(layer_kernel, out_shape=(jax.ShapeDtypeStruct((ROWS, D), B...  74 us
    unnamed x3, local copies, waits for them, and re-layouts  4.91 us

profile of v2, /device:TPU:24, one launch (start us, length us, event | category | flops | bytes accessed | tf_op | source)
XLA Modules:
  0.0 79.6 jit_solution(3375912237125884449)
XLA Ops:
  0.6 74.0 %layer.1 = (bf16[192,1024]{1,0:T(8,128)(2,1)}, bf16[192,1024]{1,0:T(8,128)(2,1)}, f32[8,1024]{1,0:T(8,128)}) custom-call(bf16[192,1024]{1,0:T(8,128)(2,1)} %tokens_in.1, s32[1,192]{1,0:T(1,128)} %hist.1, bf16[1024,4096]{1,0:T(8,128)(2,1)} %w_in.1, bf16[1024,1024]{1,0:T(8,128)(2,1)} %w_out_in.1, bf16[192,1024]{1,0:T(8,128)(2,1)} %grad_out_in.1), custom_call_target="tpu_custom_call" | custom-call | tf_op jit(solution)/shard_map/layer/pallas_call | solution.py:552
  74.7 1.8 %copy.11 = bf16[192,1024]{1,0:T(8,128)(2,1)} copy(bf16[192,1024]{1,0:T(8,128)(2,1)} %get-tuple-element.6) | data formatting | bytes 786432
  76.5 1.8 %copy.12 = bf16[192,1024]{1,0:T(8,128)(2,1)} copy(bf16[192,1024]{1,0:T(8,128)(2,1)} %get-tuple-element.7) | data formatting | bytes 786432
  78.2 1.4 %copy.13 = f32[8,1024]{1,0:T(8,128)} copy(f32[8,1024]{1,0:T(8,128)} %get-tuple-element.8) | data formatting | bytes 65536

commit v3 on v2

v3 whole, which is shorter than its diff:
```python
import jax
import jax.numpy as jnp
from jax import lax
from jax.experimental import pallas as pl
from jax.experimental.pallas import tpu as pltpu
from jax.sharding import PartitionSpec as P

HEADS = 8
HEAD = 128
ROWS = 192
HALF = 96
D = 1024
CTX = 16
G = 4 * HALF
EPS = 1e-05
SCALE = HEAD ** (-0.5)
VMEM_LIMIT = 60 * 1024 * 1024
F32 = jnp.float32
BF16 = jnp.bfloat16
U_COL, V_COL, Q_COL, K_COL = 0, D, 2 * D, 3 * D
KEY, QUERY, VALUE, GNORM = 0, 1, 2, 3

TILES = [(0, 0, 0, 0), (0, 0, 0, 1)]
TILES += [(1, 0, 0, g) for g in range(4)] + [(1, 0, 1, g) for g in range(4)]
TILES += [(0, 1, 0, g) for g in range(4)]
TILES += [(1, 1, 0, g) for g in range(4)] + [(1, 1, 1, g) for g in (2, 3)]
FIRST = {(0, 0, 0): 0, (1, 0, 0): 2, (1, 0, 1): 6, (0, 1, 0): 10, (1, 1, 0): 14, (1, 1, 1): 16}


def norm_rows(matrix):
    average = jnp.mean(matrix, axis=-1, keepdims=True)
    centred = matrix - average
    inverse = lax.rsqrt(jnp.mean(centred * centred, axis=-1, keepdims=True) + EPS)
    return centred * inverse, inverse


def norm_back(gradient, normed, inverse):
    first = jnp.mean(gradient, axis=-1, keepdims=True)
    second = jnp.mean(gradient * normed, axis=-1, keepdims=True)
    return (gradient - first - normed * second) * inverse


def dot_nt(left, right):
    return lax.dot_general(left, right, (((1,), (1,)), ((), ())), preferred_element_type=F32)


def dot_tn(left, right):
    return lax.dot_general(left, right, (((0,), (0,)), ((), ())), preferred_element_type=F32)


def dot_nn(left, right):
    return lax.dot_general(left, right, (((1,), (0,)), ((), ())), preferred_element_type=F32)


def flat(blocks):
    return blocks.reshape(-1, HEAD)


class Place:
    def __init__(self):
        self.dp = lax.axis_index("dp")
        self.t = lax.axis_index("ctx")
        self.plane = 2 * (self.dp // 2)
        self.core = self.dp % 2
        self.z = self.dp // 2
        self.sibling = {"dp": self.plane + 1 - self.core}
        self.head = self.t % HEADS
        self.slot = self.t // 2

    def worker(self, head):
        return self.plane + self.t % 2, self.core * HEADS + head

    def owner(self, i):
        return self.plane + self.t // HEADS, 2 * i + self.core

    def is_me(self, device):
        return (device[0] == self.dp) & (device[1] == self.t)

    def has_self(self):
        return (self.t % 2 == self.core) & (self.t // HEADS == self.core)


def ident(device):
    return {"dp": device[0], "ctx": device[1]}


def signal_if_other(place, barrier, device):
    @pl.when(jnp.logical_not(place.is_me(device)))
    def _():
        pl.semaphore_signal(barrier, inc=1, device_id=ident(device))


def start_copy(place, device, src, dst, send_sem, recv_sem):
    mine = place.is_me(device)

    @pl.when(mine)
    def _():
        pltpu.make_async_copy(src, dst, recv_sem).start()

    @pl.when(jnp.logical_not(mine))
    def _():
        pltpu.make_async_remote_copy(
            src, dst, send_sem, recv_sem, device_id=ident(device)
        ).start()


def wait_sent(place, ref, sem):
    pltpu.make_async_remote_copy(ref, ref, sem, sem, device_id=place.sibling).wait_send()


def wait_sent_eight(place, ref, sem):
    @pl.when(place.has_self())
    def _():
        wait_sent(place, ref.at[0:7], sem)

    @pl.when(jnp.logical_not(place.has_self()))
    def _():
        wait_sent(place, ref, sem)


def wait_arrived(dst, recv_sem):
    pltpu.make_async_copy(dst, dst, recv_sem).wait()


def history_masks(hist_all, khist, qhist, core):
    for half in range(2):
        lanes = slice(half * 128, half * 128 + HALF)
        for g in range(4):
            row = jnp.concatenate(
                [hist_all[n // 2, 2 * g + n % 2, :, lanes] for n in range(4)], axis=1
            )
            rows = jnp.broadcast_to(row.astype(F32).astype(BF16), (16, G))
            khist[half, g] = dot_tn(rows, jnp.full((16, 128), 1.0 / 16, BF16))
        for g in range(2):
            row = jnp.concatenate(
                [hist_all[core, 4 * g + n, :, lanes] for n in range(4)], axis=1
            )
            qhist[half, g] = row.astype(F32)


def query_positions(half, g, core):
    lane = lax.broadcasted_iota(jnp.int32, (1, G), 1)
    inside = lane // HALF
    block = 8 * g + 2 * inside + core
    return (31 - block if half else block) * HALF + lane - inside * HALF


def key_positions(half, g):
    row = lax.broadcasted_iota(jnp.int32, (G, 128), 0)
    inside = row // HALF
    block = 4 * g + 2 * (inside % 2) + inside // 2
    return (31 - block if half else block) * HALF + row - inside * HALF


def key_rows(got, half, g):
    return jnp.concatenate([flat(got[half, n, pl.ds(2 * g, 2)]) for n in range(2)], axis=0)


def three(matrix):
    return jnp.concatenate([matrix, matrix, matrix], axis=1)


def score_tile(n, q_got, k_got, khist, qhist, p_buf, s_buf, core):
    qh, qg, kh, kg = TILES[n]
    half = dot_nt(
        key_rows(k_got, kh, kg), flat(q_got[qh, 4 * qg : 4 * qg + 4])
    ) * (0.5 * SCALE)
    up = 1.0 + jnp.tanh(half)
    weights = half * up
    slope = weights + (0.5 * up) * (1.0 - weights)
    visible = three(khist[kh, kg]) == qhist[qh, qg]
    if qh == kh and kg // 2 == qg:
        visible = visible & (three(key_positions(kh, kg)) <= query_positions(qh, qg, core))
    p_buf[n] = jnp.where(visible, weights, 0.0).astype(BF16)
    s_buf[n] = jnp.where(visible, slope, 0.0).astype(BF16)


def mix_tiles(qh, qg, vt, p_buf):
    total = None
    for n, tile in enumerate(TILES):
        if tile[:2] == (qh, qg):
            part = dot_nn(vt[tile[2], tile[3]], p_buf[n])
            total = part if total is None else total + part
    return total


def back_tile(tile, n, q_got, v_got, kt, dot_buf, p_buf, s_buf, dqt):
    qh, qg, kh, kg = tile
    grads = dot_buf[qh, qg]
    grad_scores = dot_nn(key_rows(v_got, kh, kg), grads) * s_buf[n].astype(F32)
    grad_scores = grad_scores.astype(BF16)
    grad_v = dot_nt(p_buf[n], grads)
    grad_k = dot_nn(grad_scores, flat(q_got[qh, 4 * qg : 4 * qg + 4]))
    dqt[qh, qg] += dot_nn(kt[kh, kg], grad_scores)
    return grad_k, grad_v


def layer_kernel(
    tokens_in, hist, w_in, w_out_in, grad_out_in,
    layer_out, grad_tokens, out_grad,
    tokens, go_all, w_buf, w_out, normed_buf, slope_buf, u_buf, gate_buf,
    hist_buf, hist_all, khist, qhist,
    send_buf, k_got, v_got, q_got, n_got,
    p_buf, s_buf, vt, kt, ot_buf, gt_buf, o_send, mixed_got, mean_send, mean_got, stats, dot_buf, dqt,
    low_buf, grads_buf, part, part_send, sib_got, ret_send, ret_got, rows_acc,
    gated_buf, gpre_buf, gd_got, g_buf, c_send, c_got, f_send, f_got,
    in_sem, w_sem, hsend, hrecv, hfsend, hfrecv, send_sem, recv_sem, fsend, frecv,
    osend, orecv, msend, mrecv, ssend, srecv, psend, precv, rsend, rrecv,
    zsend, zrecv, gfsend, gfrecv, gdsend, gdrecv, csend, crecv, fin_send, fin_recv,
):
    place = Place()
    core, t, z, my_head, slot, dp = place.core, place.t, place.z, place.head, place.slot, place.dp

    t_copy = pltpu.make_async_copy(tokens_in, tokens, in_sem.at[0])
    t_copy.start()
    chunks = [K_COL, K_COL + 512, Q_COL, Q_COL + 512, V_COL, V_COL + 512, U_COL, U_COL + 512]

    def w_copy(n):
        cols = pl.ds(chunks[n], 512)
        return pltpu.make_async_copy(w_in.at[:, cols], w_buf.at[:, cols], w_sem.at[n])

    for n in range(2):
        w_copy(n).start()
    go_copy = pltpu.make_async_copy(grad_out_in, go_all.at[dp], in_sem.at[1])
    go_copy.start()
    for n in range(2, 8):
        w_copy(n).start()
    wo_copy = pltpu.make_async_copy(w_out_in, w_out, in_sem.at[2])
    wo_copy.start()

    barrier = pltpu.get_barrier_semaphore()
    for n in range(8):
        signal_if_other(place, barrier, place.owner(n))
        signal_if_other(place, barrier, place.worker(n))
    for n in range(1, 8):
        pl.semaphore_signal(barrier, inc=1, device_id={"dp": (dp + n) % 8})
    for n in range(1, CTX):
        pl.semaphore_signal(barrier, inc=1, device_id={"ctx": (t + n) % CTX})

    hist_buf[...] = jnp.zeros_like(hist_buf)
    hist_buf[:, 0:HALF] = hist[:, 0:HALF]
    hist_buf[:, 128 : 128 + HALF] = hist[:, HALF:ROWS]
    t_copy.wait()
    normed_buf[...] = norm_rows(tokens[...].astype(F32))[0].astype(BF16)

    def send_args(kind, head, half):
        got = (k_got, q_got, v_got, n_got)[kind]
        dst = got.at[half, t % 2, slot] if kind in (KEY, VALUE) else got.at[half, slot]
        batch = slot // 4 if kind in (KEY, VALUE) else 0
        return (
            place.worker(head), send_buf.at[kind, half, head], dst,
            send_sem.at[kind, half], recv_sem.at[kind, half, batch],
        )

    def hist_args(head):
        return place.worker(head), hist_buf, hist_all.at[t % 2, slot], hsend, hrecv

    def go_along(n):
        ref = go_all.at[dp]
        return pltpu.make_async_remote_copy(
            ref, ref, zsend.at[n - 1], zrecv.at[n - 1], device_id={"dp": (dp + 2 * n) % 8}
        )

    def go_across(n):
        ref = go_all.at[(dp + 8 - 2 * n) % 8]
        return pltpu.make_async_remote_copy(
            ref, ref, gfsend.at[n], gfrecv.at[n], device_id=place.sibling
        )

    def project(n):
        w_copy(n).wait()
        cols = slice(chunks[n], chunks[n] + 512)
        half = 0.5 * dot_nn(normed_buf[...], w_buf[:, cols])
        up = 1.0 + jnp.tanh(half)
        act = half * up
        slope_buf[:, cols] = act + (0.5 * up) * (1.0 - act)
        return act.astype(BF16)

    for n in range(8):
        act = project(n)
        if n == 0:
            pl.semaphore_wait(barrier, 16 + 7 + 15 - 2 * place.has_self().astype(jnp.int32))
            for head in range(HEADS):
                start_copy(place, *hist_args(head))
        if n < 6:
            for j in range(4):
                head = (n % 2) * 4 + j
                for half in range(2):
                    send_buf[n // 2, half, head] = act[
                        half * HALF : (half + 1) * HALF, j * 128 : (j + 1) * 128
                    ]
                start_copy(place, *send_args(n // 2, head, 0))
        else:
            u_buf[:, chunks[n] : chunks[n] + 512] = act

    go_copy.wait()
    wo_copy.wait()
    gate_buf[...] = dot_nt(go_all[dp], w_out[...])
    grad_norm = (gate_buf[...] * u_buf[...].astype(F32)).astype(BF16)
    for head in range(HEADS):
        for half in range(2):
            send_buf[GNORM, half, head] = grad_norm[
                half * HALF : (half + 1) * HALF, head * 128 : (head + 1) * 128
            ]
        start_copy(place, *send_args(GNORM, head, 0))
    for kind in (QUERY, KEY, VALUE, GNORM):
        for head in range(HEADS):
            start_copy(place, *send_args(kind, head, 1))
    for n in (2, 1, 3):
        go_along(n).start()
    go_across(0).start()

    def hist_forward():
        ref = hist_all.at[core]
        return pltpu.make_async_remote_copy(ref, ref, hfsend, hfrecv, device_id=place.sibling)

    def forward(kind, half, batch):
        ref = (k_got, None, v_got)[kind].at[half, core, 4 * batch : 4 * batch + 4]
        return pltpu.make_async_remote_copy(
            ref, ref, fsend.at[kind // 2, half, batch], frecv.at[kind // 2, half, batch],
            device_id=place.sibling,
        )

    def pass_on(kind, half):
        got = (k_got, None, v_got)[kind]
        for batch in range(2):
            wait_arrived(
                got.at[half, core, 4 * batch : 4 * batch + 4], recv_sem.at[kind, half, batch]
            )
            forward(kind, half, batch).start()

    def wait_passed(kind, half):
        for batch in range(2):
            forward(kind, half, batch).wait_recv()

    def wait_rows(kind, half):
        got = (None, q_got, None, n_got)[kind]
        wait_arrived(got.at[half], recv_sem.at[kind, half, 0])

    wait_arrived(hist_all.at[core], hrecv)
    hist_forward().start()
    hist_forward().wait_recv()
    history_masks(hist_all, khist, qhist, core)

    def scores(qh, kh):
        for n, tile in enumerate(TILES):
            if (tile[0], tile[2]) == (qh, kh):
                score_tile(n, q_got, k_got, khist, qhist, p_buf, s_buf, core)

    def mean_args(i):
        return place.owner(i), mean_send.at[i], mean_got.at[my_head], msend, mrecv

    def o_args(i, half):
        return (
            place.owner(i), o_send.at[half, i], mixed_got.at[half, my_head],
            osend.at[half], orecv.at[half],
        )

    def mix(qh):
        for g in range(4):
            vt[qh, g] = key_rows(v_got, qh, g).T
        for qg in range(2):
            mixed_t = mix_tiles(qh, qg, vt, p_buf)
            average = jnp.mean(mixed_t, axis=0, keepdims=True)
            centred = mixed_t - average
            ot_buf[qh, qg] = centred
            o_send[qh, 4 * qg : 4 * qg + 4] = centred.T.astype(BF16).reshape(4, HALF, HEAD)
            for n in range(4):
                mean_send[4 * qg + n, :, qh * 128 : qh * 128 + HALF] = average[
                    :, n * HALF : (n + 1) * HALF
                ]
            stats[my_head, qh, 4 * qg : 4 * qg + 1] = average
            stats[my_head, qh, 4 * qg + 1 : 4 * qg + 2] = jnp.sum(
                centred * centred, axis=0, keepdims=True
            )

    def stats_copy(qh, n):
        there = (t // HEADS) * HEADS + (my_head + n) % HEADS
        ref = stats.at[my_head, qh]
        return pltpu.make_async_remote_copy(
            ref, ref, ssend.at[qh], srecv.at[qh], device_id={"ctx": there}
        )

    def send_stats(qh):
        wait_rows(GNORM, qh)
        for qg in range(2):
            grad_t = flat(n_got[qh, 4 * qg : 4 * qg + 4]).T
            gt_buf[qh, qg] = grad_t
            grad_t = grad_t.astype(F32)
            stats[my_head, qh, 4 * qg + 2 : 4 * qg + 3] = jnp.sum(grad_t, axis=0, keepdims=True)
            stats[my_head, qh, 4 * qg + 3 : 4 * qg + 4] = jnp.sum(
                grad_t * ot_buf[qh, qg], axis=0, keepdims=True
            )
        for n in range(1, HEADS):
            stats_copy(qh, n).start()

    def grads_of_mixed(qh):
        wait_arrived(stats.at[0:7, qh], srecv.at[qh])
        for qg in range(2):
            rows = [
                [stats[h, qh, 4 * qg + k : 4 * qg + k + 1] for h in range(HEADS)] for k in range(4)
            ]
            average = sum(rows[0]) * (1.0 / HEADS)
            off = [row - average for row in rows[0]]
            spread = sum(rows[1]) + HEAD * sum(o * o for o in off)
            inverse = lax.rsqrt(spread * (1.0 / D) + EPS)
            first = sum(rows[2]) * (1.0 / D)
            second = (sum(rows[3]) + sum(o * a for o, a in zip(off, rows[2]))) * (1.0 / D)
            centred = ot_buf[qh, qg] + (stats[my_head, qh, 4 * qg : 4 * qg + 1] - average)
            dot_buf[qh, qg] = (
                (gt_buf[qh, qg].astype(F32) - first - centred * (second * inverse * inverse))
                * inverse
            ).astype(BF16)

    def turn_keys(half):
        for g in range(4):
            kt[half, g] = key_rows(k_got, half, g).T

    def part_copy(kind, kg, kh):
        ref = part_send.at[kind, kg, kh]
        return pltpu.make_async_remote_copy(
            ref, sib_got.at[kind, kg, kh], psend.at[kind, kg, kh], precv.at[kind, kg, kh],
            device_id=place.sibling,
        )

    def ret_args(kind, i, half):
        return (
            place.owner(i), ret_send.at[kind, half, i], ret_got.at[kind, half, my_head],
            rsend.at[kind, half], rrecv.at[kind, half],
        )

    def back(qh, qg, kh, kg):
        n = FIRST[qh, qg, kh] + kg
        return back_tile(
            (qh, qg, kh, kg), n, q_got, v_got, kt, dot_buf, p_buf, s_buf, dqt
        )

    def back_lower():
        for kg in range(4):
            grad_k, grad_v = back(0, 1, 0, kg)
            if kg < 2:
                term_k, term_v = back(0, 0, 0, kg)
                grad_k, grad_v = grad_k + term_k, grad_v + term_v
            low_buf[0, kg], low_buf[1, kg] = grad_k, grad_v

    def group_at(step):
        return (step + t) % 4

    def back_part(step, kh):
        kg = group_at(step)
        grad_k, grad_v = back(1, 0, kh, kg)
        if kh == 0:
            term_k, term_v = back(1, 1, kh, kg)
            grads_buf[0] = (grad_k + term_k) + low_buf[0, kg]
            grads_buf[1] = (grad_v + term_v) + low_buf[1, kg]
        else:
            grads_buf[0], grads_buf[1] = grad_k, grad_v

            @pl.when(kg >= 2)
            def _():
                term_k, term_v = back(1, 1, kh, kg)
                grads_buf[0] += term_k
                grads_buf[1] += term_v

        for kind in (1, 0):
            grad = grads_buf[kind] * SCALE if kind == 0 else grads_buf[kind]
            grad = grad.reshape(2, 2, HALF, HEAD)
            for parity in range(2):
                part[kind, step, kh, parity] = grad[parity]
            part_send[kind, step, kh] = part[kind, step, kh, 1 - core].astype(BF16)
            part_copy(kind, step, kh).start()

    def return_part(step, kh):
        kg = group_at(step)
        for kind in (1, 0):
            part_copy(kind, step, kh).wait_recv()
            total = part[kind, step, kh, core] + sib_got[kind, step, kh].astype(F32)
            for n in range(2):
                ret_send[kind, kh, 2 * kg + n] = total[n].astype(BF16)
                start_copy(place, *ret_args(kind, 2 * kg + n, kh))

    def return_queries(qg, qh):
        grad_q = (dqt[qh, qg] * SCALE).T.astype(BF16).reshape(4, HALF, HEAD)
        for n in range(4):
            ret_send[2, qh, 4 * qg + n] = grad_q[n]
            start_copy(place, *ret_args(2, 4 * qg + n, qh))

    mean_send[...] = jnp.zeros_like(mean_send)
    dqt[...] = jnp.zeros_like(dqt)
    pass_on(KEY, 0)
    wait_rows(QUERY, 0)
    wait_passed(KEY, 0)
    scores(0, 0)
    pass_on(VALUE, 0)
    turn_keys(0)
    wait_passed(VALUE, 0)
    mix(0)
    send_stats(0)
    wait_rows(QUERY, 1)
    scores(1, 0)
    pass_on(KEY, 1)
    grads_of_mixed(0)
    wait_passed(KEY, 1)
    scores(1, 1)
    pass_on(VALUE, 1)
    for i in range(8):
        start_copy(place, *o_args(i, 0))
    back_lower()
    wait_passed(VALUE, 1)
    mix(1)
    send_stats(1)
    for i in range(8):
        start_copy(place, *mean_args(i))
        start_copy(place, *o_args(i, 1))
    return_queries(0, 0)
    return_queries(1, 0)
    turn_keys(1)
    for n in range(1, 4):
        wait_arrived(go_all.at[(dp + 8 - 2 * n) % 8], zrecv.at[n - 1])
        go_across(n).start()
    grads_of_mixed(1)

    def gated_copy(n):
        there = (dp + n) % 8
        cols = pl.ds(pl.multiple_of(there * 128, 128), 128)
        return pltpu.make_async_remote_copy(
            gated_buf.at[:, cols], gd_got.at[dp], gdsend, gdrecv,
            device_id={"dp": there},
        )

    def gate():
        wait_arrived(mean_got, mrecv)
        for half in range(2):
            wait_arrived(mixed_got.at[half], orecv.at[half])
        means = mean_got[...].reshape(HEADS, 256).T
        means = jnp.concatenate([means[0:HALF], means[128 : 128 + HALF]], axis=0)
        mixed = jnp.concatenate(
            [
                flat(mixed_got[:, head]).astype(F32) + means[:, head : head + 1]
                for head in range(HEADS)
            ],
            axis=1,
        )
        mixed_n, _ = norm_rows(mixed)
        gated_buf[...] = (mixed_n * u_buf[...].astype(F32)).astype(BF16)
        for n in range(1, 8):
            gated_copy(n).start()
        gd_got[dp] = gated_buf[:, pl.ds(pl.multiple_of(dp * 128, 128), 128)]
        gpre_buf[...] = (gate_buf[...] * mixed_n * slope_buf[:, U_COL : U_COL + D]).astype(BF16)

    def to_ctx(n):
        there = (t + n) % CTX
        return pltpu.make_async_remote_copy(
            c_send.at[there], c_got.at[n - 1], csend, crecv,
            device_id={"ctx": there},
        )

    def product():
        for n in range(4):
            wait_arrived(go_all.at[(place.sibling["dp"] + 8 - 2 * n) % 8], gfrecv.at[n])
        wait_arrived(gd_got.at[0:7], gdrecv)
        total = dot_tn(gd_got[...].reshape(8 * ROWS, 128), go_all[...].reshape(8 * ROWS, D)).T
        total = total.reshape(8, CTX, 8, 128)
        for there in range(CTX):
            piece = total[:, there].reshape(64, 128)
            g_buf[there] = piece
            c_send[there] = piece.astype(BF16)
        for n in range(1, CTX):
            to_ctx(n).start()

    def fin_copy(n):
        there = (dp + n) % 8
        return pltpu.make_async_remote_copy(
            f_send.at[there], f_got.at[dp], fin_send, fin_recv,
            device_id={"dp": there},
        )

    def sum_places():
        wait_arrived(c_got, crecv)
        total = g_buf[t]
        for n in range(1, CTX):
            total = total + c_got[n - 1].astype(F32)
        f_send[...] = (total * (24576.0 ** (-0.5))).reshape(8, 8, 128)
        for n in range(1, 8):
            fin_copy(n).start()
        f_got[dp] = f_send[dp]

    back_part(0, 0)
    back_part(0, 1)
    return_part(0, 0)
    gate()
    back_part(1, 0)
    return_part(0, 1)
    back_part(1, 1)
    return_part(1, 0)
    back_part(2, 0)
    return_part(1, 1)
    back_part(2, 1)
    return_part(2, 0)
    product()
    back_part(3, 0)
    return_part(2, 1)
    back_part(3, 1)
    return_part(3, 0)
    return_queries(0, 1)
    return_queries(1, 1)
    return_part(3, 1)

    layer_out[...] = (dot_nn(gated_buf[...], w_out[...]) + tokens[...].astype(F32)).astype(BF16)
    rows_acc[...] = dot_nt(gpre_buf[...], w_buf[:, U_COL : U_COL + D])

    def rows_part(kind, col):
        for half in range(2):
            wait_arrived(ret_got.at[kind, half], rrecv.at[kind, half])
        gradient = jnp.concatenate([flat(ret_got[kind, :, head]) for head in range(HEADS)], axis=1)
        grad_pre = (gradient.astype(F32) * slope_buf[:, col : col + D]).astype(BF16)
        rows_acc[...] += dot_nt(grad_pre, w_buf[:, col : col + D])

    rows_part(1, V_COL)
    sum_places()
    rows_part(0, K_COL)
    rows_part(2, Q_COL)

    normed, inv_x = norm_rows(tokens[...].astype(F32))
    grad_tokens[...] = (
        go_all[dp].astype(F32) + norm_back(rows_acc[...], normed, inv_x)
    ).astype(BF16)

    wait_arrived(f_got.at[0:7], fin_recv)
    for n in range(8):
        out_grad[:, n * 128 : (n + 1) * 128] = f_got[n]

    for n in range(1, 4):
        go_along(n).wait_send()
    for n in range(4):
        go_across(n).wait_send()
    wait_sent(place, gd_got.at[0:7], gdsend)
    wait_sent(place, f_got.at[0:7], fin_send)
    wait_sent(place, c_got, csend)
    hist_forward().wait_send()
    wait_sent_eight(place, hist_all.at[core], hsend)
    wait_sent_eight(place, mean_send, msend)
    for half in range(2):
        wait_sent(place, stats.at[0:7, half], ssend.at[half])
        wait_sent_eight(place, o_send.at[half], osend.at[half])
        for kind in range(4):
            wait_sent_eight(place, send_buf.at[kind, half], send_sem.at[kind, half])
        for kind in range(3):
            wait_sent_eight(place, ret_send.at[kind, half], rsend.at[kind, half])
        for kind in (KEY, VALUE):
            for batch in range(2):
                forward(kind, half, batch).wait_send()
    for kind in range(2):
        for kg in range(4):
            for kh in range(2):
                part_copy(kind, kg, kh).wait_send()


def copy_kernel(*refs):
    for source, target in zip(refs[:3], refs[3:]):
        target[...] = source[...]


def copied(arrays):
    vmem_spec = pl.BlockSpec(memory_space=pltpu.VMEM)
    return pl.pallas_call(
        copy_kernel,
        out_shape=tuple(jax.ShapeDtypeStruct(a.shape, a.dtype) for a in arrays),
        in_specs=[vmem_spec] * 3,
        out_specs=(vmem_spec,) * 3,
        name="results",
    )(*arrays)


def on_device(tokens, segments, w_in, w_out, grad_out):
    any_spec = pl.BlockSpec(memory_space=pl.ANY)
    vmem_spec = pl.BlockSpec(memory_space=pltpu.VMEM)
    dma = pltpu.SemaphoreType.DMA
    vmem = pltpu.VMEM
    tiles = len(TILES)
    results = pl.pallas_call(
        layer_kernel,
        out_shape=(
            jax.ShapeDtypeStruct((ROWS, D), BF16),
            jax.ShapeDtypeStruct((ROWS, D), BF16),
            jax.ShapeDtypeStruct((8, D), F32),
        ),
        in_specs=[any_spec, vmem_spec, any_spec, any_spec, any_spec],
        out_specs=(vmem_spec, vmem_spec, vmem_spec),
        scratch_shapes=[
            vmem((ROWS, D), BF16),
            vmem((8, ROWS, D), BF16),
            vmem((D, 4 * D), BF16),
            vmem((D, D), BF16),
            vmem((ROWS, D), BF16),
            vmem((ROWS, 4 * D), F32),
            vmem((ROWS, D), BF16),
            vmem((ROWS, D), F32),
            vmem((1, 256), jnp.int32),
            vmem((2, 8, 1, 256), jnp.int32),
            vmem((2, 4, G, 128), F32),
            vmem((2, 2, 1, G), F32),
            vmem((4, 2, HEADS, HALF, HEAD), BF16),
            vmem((2, 2, 8, HALF, HEAD), BF16),
            vmem((2, 2, 8, HALF, HEAD), BF16),
            vmem((2, 8, HALF, HEAD), BF16),
            vmem((2, 8, HALF, HEAD), BF16),
            vmem((tiles, G, G), BF16),
            vmem((tiles, G, G), BF16),
            vmem((2, 4, HEAD, G), BF16),
            vmem((2, 4, HEAD, G), BF16),
            vmem((2, 2, HEAD, G), F32),
            vmem((2, 2, HEAD, G), BF16),
            vmem((2, 8, HALF, HEAD), BF16),
            vmem((2, HEADS, HALF, HEAD), BF16),
            vmem((8, 1, 256), F32),
            vmem((HEADS, 1, 256), F32),
            vmem((HEADS, 2, 8, G), F32),
            vmem((2, 2, HEAD, G), BF16),
            vmem((2, 2, HEAD, G), F32),
            vmem((2, 4, G, HEAD), F32),
            vmem((2, G, HEAD), F32),
            vmem((2, 4, 2, 2, 2, HALF, HEAD), F32),
            vmem((2, 4, 2, 2, HALF, HEAD), BF16),
            vmem((2, 4, 2, 2, HALF, HEAD), BF16),
            vmem((3, 2, 8, HALF, HEAD), BF16),
            vmem((3, 2, HEADS, HALF, HEAD), BF16),
            vmem((ROWS, D), F32),
            vmem((ROWS, D), BF16),
            vmem((ROWS, D), BF16),
            vmem((8, ROWS, 128), BF16),
            vmem((CTX, 64, 128), F32),
            vmem((CTX, 64, 128), BF16),
            vmem((CTX - 1, 64, 128), BF16),
            vmem((8, 8, 128), F32),
            vmem((8, 8, 128), F32),
            dma((3,)), dma((8,)),
            dma, dma, dma, dma,
            dma((4, 2)), dma((4, 2, 2)), dma((2, 2, 2)), dma((2, 2, 2)),
            dma((2,)), dma((2,)), dma, dma,
            dma((2,)), dma((2,)),
            dma((2, 4, 2)), dma((2, 4, 2)), dma((3, 2)), dma((3, 2)),
            dma((3,)), dma((3,)), dma((4,)), dma((4,)),
            dma, dma, dma, dma,
            dma, dma,
        ],
        compiler_params=pltpu.CompilerParams(
            collective_id=0, has_side_effects=True, vmem_limit_bytes=VMEM_LIMIT
        ),
        name="layer",
    )(tokens, segments, w_in, w_out, grad_out)
    return copied(results)


def solution(mesh):
    return jax.shard_map(
        on_device,
        mesh=mesh,
        in_specs=(P(("dp", "ctx"), None), P("dp", "ctx"), P(), P(), P(("dp", "ctx"), None)),
        out_specs=(P(("dp", "ctx"), None), P(("dp", "ctx"), None), P(("dp", "ctx"), None)),
        check_vma=False,
    )
```

time: 79.9 us -> 71.2 us (0.89)
  the two profiles are of different devices: /device:TPU:24 before, /device:TPU:1 now
where the time goes in v3:
time: 71.2 us; the launch traced here: 71.1 us
  Pallas kernels  70.4 us (99%)
    pallas_call x1, Pallas kernels, on_device(): pl.pallas_call(layer_kernel, out_shape=(jax.ShapeDtypeStruct((ROWS, D), B...  68.4 us
    pallas_call x1, Pallas kernels, copied(): pl.pallas_call(copy_kernel, out_shape=tuple((jax.ShapeDtypeStruct(a.shape...  2.02 us

profile of v3, /device:TPU:1, one launch (start us, length us, event | category | flops | bytes accessed | tf_op | source)
XLA Modules:
  0.0 71.1 jit_solution(15083616894249531957)
XLA Ops:
  0.6 68.4 %layer.1 = (bf16[192,1024]{1,0:T(8,128)(2,1)}, bf16[192,1024]{1,0:T(8,128)(2,1)}, f32[8,1024]{1,0:T(8,128)}) custom-call(bf16[192,1024]{1,0:T(8,128)(2,1)} %tokens_in.1, s32[1,192]{1,0:T(1,128)} %hist.1, bf16[1024,4096]{1,0:T(8,128)(2,1)} %w_in.1, bf16[1024,1024]{1,0:T(8,128)(2,1)} %w_out_in.1, bf16[192,1024]{1,0:T(8,128)(2,1)} %grad_out_in.1), custom_call_target="tpu_custom_call" | custom-call | tf_op jit(solution)/shard_map/layer/pallas_call | solution.py:681
  69.0 2.0 %results.1 = (bf16[192,1024]{1,0:T(8,128)(2,1)}, bf16[192,1024]{1,0:T(8,128)(2,1)}, f32[8,1024]{1,0:T(8,128)}) custom-call(bf16[192,1024]{1,0:T(8,128)(2,1)} %get-tuple-element.6.refs_0_, bf16[192,1024]{1,0:T(8,128)(2,1)} %get-tuple-element.7.refs_1_, f32[8,1024]{1,0:T(8,128)} %get-tuple-element.8.refs_2_), custom_call_target="tpu_custom_call" | custom-call | tf_op jit(solution)/shard_map/results/pallas_call | solution.py:666

commit v4 on v3

--- a/solution.py
+++ b/solution.py
@@ -14,6 +14,7 @@
 G = 4 * HALF
 EPS = 1e-05
 SCALE = HEAD ** (-0.5)
+FAR = -float(2**30)
 VMEM_LIMIT = 60 * 1024 * 1024
 F32 = jnp.float32
 BF16 = jnp.bfloat16
@@ -90,18 +91,25 @@
         pl.semaphore_signal(barrier, inc=1, device_id=ident(device))
 
 
-def start_copy(place, device, src, dst, send_sem, recv_sem):
-    mine = place.is_me(device)
-
-    @pl.when(mine)
+def send(device, src, dst, send_sem, recv_sem):
+    pltpu.make_async_remote_copy(src, dst, send_sem, recv_sem, device_id=ident(device)).start()
+
+
+def keep(device, src, dst, send_sem, recv_sem):
+    pltpu.make_async_copy(src, dst, recv_sem).start()
+
+
+def send_eight(place, first, args):
+    @pl.when(place.has_self())
     def _():
-        pltpu.make_async_copy(src, dst, recv_sem).start()
-
-    @pl.when(jnp.logical_not(mine))
+        keep(*args(first))
+
+    @pl.when(jnp.logical_not(place.has_self()))
     def _():
-        pltpu.make_async_remote_copy(
-            src, dst, send_sem, recv_sem, device_id=ident(device)
-        ).start()
+        send(*args(first))
+
+    for n in range(1, 8):
+        send(*args((first + n) % 8))
 
 
 def wait_sent(place, ref, sem):
@@ -122,20 +130,24 @@
     pltpu.make_async_copy(dst, dst, recv_sem).wait()
 
 
-def history_masks(hist_all, khist, qhist, core):
+def history_masks(hist_all, k_hist, q_hist, core):
+    lane = lax.broadcasted_iota(jnp.int32, (G, 128), 1).astype(F32)
+
+    def numbers(blocks):
+        rows = jnp.broadcast_to(
+            jnp.concatenate(blocks, axis=1).astype(F32).astype(BF16), (16, G)
+        )
+        return dot_tn(rows, jnp.full((16, 128), 1.0 / 16, BF16))
+
     for half in range(2):
         lanes = slice(half * 128, half * 128 + HALF)
         for g in range(4):
-            row = jnp.concatenate(
-                [hist_all[n // 2, 2 * g + n % 2, :, lanes] for n in range(4)], axis=1
-            )
-            rows = jnp.broadcast_to(row.astype(F32).astype(BF16), (16, G))
-            khist[half, g] = dot_tn(rows, jnp.full((16, 128), 1.0 / 16, BF16))
+            number = numbers([hist_all[n // 2, 2 * g + n % 2, :, lanes] for n in range(4)])
+            other = (lane < 8.0) & (number != lane)
+            k_hist[half, g] = jnp.where(other, FAR, 0.0).astype(BF16)
         for g in range(2):
-            row = jnp.concatenate(
-                [hist_all[core, 4 * g + n, :, lanes] for n in range(4)], axis=1
-            )
-            qhist[half, g] = row.astype(F32)
+            number = numbers([hist_all[core, 4 * g + n, :, lanes] for n in range(4)])
+            q_hist[half, g] = jnp.where(number == lane, 1.0, 0.0).astype(BF16)
 
 
 def query_positions(half, g, core):
@@ -160,25 +172,26 @@
     return jnp.concatenate([matrix, matrix, matrix], axis=1)
 
 
-def score_tile(n, q_got, k_got, khist, qhist, p_buf, s_buf, core):
+def score_tile(n, q_got, k_got, k_hist, q_hist, p_buf, s_buf, core):
     qh, qg, kh, kg = TILES[n]
-    half = dot_nt(
-        key_rows(k_got, kh, kg), flat(q_got[qh, 4 * qg : 4 * qg + 4])
-    ) * (0.5 * SCALE)
+    keys = jnp.concatenate([key_rows(k_got, kh, kg), k_hist[kh, kg]], axis=1)
+    queries = jnp.concatenate([flat(q_got[qh, 4 * qg : 4 * qg + 4]), q_hist[qh, qg]], axis=1)
+    half = dot_nt(keys, queries) * (0.5 * SCALE)
     up = 1.0 + jnp.tanh(half)
     weights = half * up
-    slope = weights + (0.5 * up) * (1.0 - weights)
-    visible = three(khist[kh, kg]) == qhist[qh, qg]
+    slope = up + weights * (2.0 - up)
     if qh == kh and kg // 2 == qg:
-        visible = visible & (three(key_positions(kh, kg)) <= query_positions(qh, qg, core))
-    p_buf[n] = jnp.where(visible, weights, 0.0).astype(BF16)
-    s_buf[n] = jnp.where(visible, slope, 0.0).astype(BF16)
-
-
-def mix_tiles(qh, qg, vt, p_buf):
+        visible = three(key_positions(kh, kg)) <= query_positions(qh, qg, core)
+        weights = jnp.where(visible, weights, 0.0)
+        slope = jnp.where(visible, slope, 0.0)
+    p_buf[n] = weights.astype(BF16)
+    s_buf[n] = slope.astype(BF16)
+
+
+def mix_tiles(qh, qg, kh, vt, p_buf):
     total = None
     for n, tile in enumerate(TILES):
-        if tile[:2] == (qh, qg):
+        if tile[:3] == (qh, qg, kh):
             part = dot_nn(vt[tile[2], tile[3]], p_buf[n])
             total = part if total is None else total + part
     return total
@@ -199,7 +212,7 @@
     tokens_in, hist, w_in, w_out_in, grad_out_in,
     layer_out, grad_tokens, out_grad,
     tokens, go_all, w_buf, w_out, normed_buf, slope_buf, u_buf, gate_buf,
-    hist_buf, hist_all, khist, qhist,
+    hist_buf, hist_all, k_hist, q_hist,
     send_buf, k_got, v_got, q_got, n_got,
     p_buf, s_buf, vt, kt, ot_buf, gt_buf, o_send, mixed_got, mean_send, mean_got, stats, dot_buf, dqt,
     low_buf, grads_buf, part, part_send, sib_got, ret_send, ret_got, rows_acc,
@@ -280,8 +293,7 @@
         act = project(n)
         if n == 0:
             pl.semaphore_wait(barrier, 16 + 7 + 15 - 2 * place.has_self().astype(jnp.int32))
-            for head in range(HEADS):
-                start_copy(place, *hist_args(head))
+            send_eight(place, my_head, hist_args)
         if n < 6:
             for j in range(4):
                 head = (n % 2) * 4 + j
@@ -289,7 +301,8 @@
                     send_buf[n // 2, half, head] = act[
                         half * HALF : (half + 1) * HALF, j * 128 : (j + 1) * 128
                     ]
-                start_copy(place, *send_args(n // 2, head, 0))
+            if n % 2:
+                send_eight(place, my_head, lambda head: send_args(n // 2, head, 0))
         else:
             u_buf[:, chunks[n] : chunks[n] + 512] = act
 
@@ -302,10 +315,9 @@
             send_buf[GNORM, half, head] = grad_norm[
                 half * HALF : (half + 1) * HALF, head * 128 : (head + 1) * 128
             ]
-        start_copy(place, *send_args(GNORM, head, 0))
+    send_eight(place, my_head, lambda head: send_args(GNORM, head, 0))
     for kind in (QUERY, KEY, VALUE, GNORM):
-        for head in range(HEADS):
-            start_copy(place, *send_args(kind, head, 1))
+        send_eight(place, my_head, lambda head: send_args(kind, head, 1))
     for n in (2, 1, 3):
         go_along(n).start()
     go_across(0).start()
@@ -340,12 +352,12 @@
     wait_arrived(hist_all.at[core], hrecv)
     hist_forward().start()
     hist_forward().wait_recv()
-    history_masks(hist_all, khist, qhist, core)
+    history_masks(hist_all, k_hist, q_hist, core)
 
     def scores(qh, kh):
         for n, tile in enumerate(TILES):
             if (tile[0], tile[2]) == (qh, kh):
-                score_tile(n, q_got, k_got, khist, qhist, p_buf, s_buf, core)
+                score_tile(n, q_got, k_got, k_hist, q_hist, p_buf, s_buf, core)
 
     def mean_args(i):
         return place.owner(i), mean_send.at[i], mean_got.at[my_head], msend, mrecv
@@ -360,7 +372,9 @@
         for g in range(4):
             vt[qh, g] = key_rows(v_got, qh, g).T
         for qg in range(2):
-            mixed_t = mix_tiles(qh, qg, vt, p_buf)
+            mixed_t = mix_tiles(qh, qg, qh, vt, p_buf)
+            if qh == 1:
+                mixed_t = mixed_t + ot_buf[qh, qg]
             average = jnp.mean(mixed_t, axis=0, keepdims=True)
             centred = mixed_t - average
             ot_buf[qh, qg] = centred
@@ -451,39 +465,59 @@
         grad_k, grad_v = back(1, 0, kh, kg)
         if kh == 0:
             term_k, term_v = back(1, 1, kh, kg)
-            grads_buf[0] = (grad_k + term_k) + low_buf[0, kg]
-            grads_buf[1] = (grad_v + term_v) + low_buf[1, kg]
+            grads_buf[0] = ((grad_k + term_k) + low_buf[0, kg]).reshape(2, ROWS, HEAD)
+            grads_buf[1] = ((grad_v + term_v) + low_buf[1, kg]).reshape(2, ROWS, HEAD)
         else:
-            grads_buf[0], grads_buf[1] = grad_k, grad_v
+            grads_buf[0] = grad_k.reshape(2, ROWS, HEAD)
+            grads_buf[1] = grad_v.reshape(2, ROWS, HEAD)
 
             @pl.when(kg >= 2)
             def _():
                 term_k, term_v = back(1, 1, kh, kg)
-                grads_buf[0] += term_k
-                grads_buf[1] += term_v
+                grads_buf[0] += term_k.reshape(2, ROWS, HEAD)
+                grads_buf[1] += term_v.reshape(2, ROWS, HEAD)
 
         for kind in (1, 0):
-            grad = grads_buf[kind] * SCALE if kind == 0 else grads_buf[kind]
-            grad = grad.reshape(2, 2, HALF, HEAD)
-            for parity in range(2):
-                part[kind, step, kh, parity] = grad[parity]
-            part_send[kind, step, kh] = part[kind, step, kh, 1 - core].astype(BF16)
+            scale = 0.5 * SCALE if kind == 0 else 1.0
+            part_send[kind, step, kh] = (
+                (grads_buf[kind, 1 - core] * scale).astype(BF16).reshape(2, HALF, HEAD)
+            )
             part_copy(kind, step, kh).start()
+            part[kind, step, kh] = (grads_buf[kind, core] * scale).reshape(2, HALF, HEAD)
 
     def return_part(step, kh):
         kg = group_at(step)
         for kind in (1, 0):
             part_copy(kind, step, kh).wait_recv()
-            total = part[kind, step, kh, core] + sib_got[kind, step, kh].astype(F32)
+            total = part[kind, step, kh] + sib_got[kind, step, kh].astype(F32)
             for n in range(2):
                 ret_send[kind, kh, 2 * kg + n] = total[n].astype(BF16)
-                start_copy(place, *ret_args(kind, 2 * kg + n, kh))
-
-    def return_queries(qg, qh):
-        grad_q = (dqt[qh, qg] * SCALE).T.astype(BF16).reshape(4, HALF, HEAD)
-        for n in range(4):
-            ret_send[2, qh, 4 * qg + n] = grad_q[n]
-            start_copy(place, *ret_args(2, 4 * qg + n, qh))
+        first, second = 2 * kg + slot % 2, 2 * kg + 1 - slot % 2
+        own = place.has_self() & (kg == slot // 2)
+
+        @pl.when(own)
+        def _():
+            for kind in (1, 0):
+                keep(*ret_args(kind, first, kh))
+
+        @pl.when(jnp.logical_not(own))
+        def _():
+            for kind in (1, 0):
+                send(*ret_args(kind, first, kh))
+
+        for kind in (1, 0):
+            send(*ret_args(kind, second, kh))
+
+    def return_queries(qh):
+        for qg in range(2):
+            grad_q = (dqt[qh, qg] * (0.5 * SCALE)).T.astype(BF16).reshape(4, HALF, HEAD)
+            for n in range(4):
+                ret_send[2, qh, 4 * qg + n] = grad_q[n]
+        send_eight(place, slot, lambda i: ret_args(2, i, qh))
+
+    def pass_grads(n):
+        wait_arrived(go_all.at[(dp + 8 - 2 * n) % 8], zrecv.at[n - 1])
+        go_across(n).start()
 
     mean_send[...] = jnp.zeros_like(mean_send)
     dqt[...] = jnp.zeros_like(dqt)
@@ -502,22 +536,21 @@
     grads_of_mixed(0)
     wait_passed(KEY, 1)
     scores(1, 1)
+    pass_grads(2)
+    turn_keys(1)
+    for qg in range(2):
+        ot_buf[1, qg] = mix_tiles(1, qg, 0, vt, p_buf)
+    back_lower()
     pass_on(VALUE, 1)
-    for i in range(8):
-        start_copy(place, *o_args(i, 0))
-    back_lower()
     wait_passed(VALUE, 1)
     mix(1)
     send_stats(1)
-    for i in range(8):
-        start_copy(place, *mean_args(i))
-        start_copy(place, *o_args(i, 1))
-    return_queries(0, 0)
-    return_queries(1, 0)
-    turn_keys(1)
-    for n in range(1, 4):
-        wait_arrived(go_all.at[(dp + 8 - 2 * n) % 8], zrecv.at[n - 1])
-        go_across(n).start()
+    send_eight(place, slot, mean_args)
+    for half in range(2):
+        send_eight(place, slot, lambda i: o_args(i, half))
+    return_queries(0)
+    for n in (1, 3):
+        pass_grads(n)
     grads_of_mixed(1)
 
     def gated_copy(n):
@@ -555,12 +588,25 @@
             device_id={"ctx": there},
         )
 
+    def fin_copy(n):
+        there = (dp + n) % 8
+        return pltpu.make_async_remote_copy(
+            f_send.at[there], f_got.at[dp], fin_send, fin_recv, device_id={"dp": there}
+        )
+
     def product():
         for n in range(4):
             wait_arrived(go_all.at[(place.sibling["dp"] + 8 - 2 * n) % 8], gfrecv.at[n])
         wait_arrived(gd_got.at[0:7], gdrecv)
         total = dot_tn(gd_got[...].reshape(8 * ROWS, 128), go_all[...].reshape(8 * ROWS, D)).T
-        total = total.reshape(8, CTX, 8, 128)
+        f_send[...] = total.reshape(8, 128, 128).astype(BF16)
+        for n in range(1, 8):
+            fin_copy(n).start()
+
+    def spread():
+        wait_arrived(f_got.at[0:7], fin_recv)
+        f_got[dp] = f_send[dp]
+        total = f_got[...].astype(F32).reshape(8, CTX, 8, 128)
         for there in range(CTX):
             piece = total[:, there].reshape(64, 128)
             g_buf[there] = piece
@@ -568,42 +614,33 @@
         for n in range(1, CTX):
             to_ctx(n).start()
 
-    def fin_copy(n):
-        there = (dp + n) % 8
-        return pltpu.make_async_remote_copy(
-            f_send.at[there], f_got.at[dp], fin_send, fin_recv,
-            device_id={"dp": there},
-        )
-
     def sum_places():
         wait_arrived(c_got, crecv)
         total = g_buf[t]
         for n in range(1, CTX):
             total = total + c_got[n - 1].astype(F32)
-        f_send[...] = (total * (24576.0 ** (-0.5))).reshape(8, 8, 128)
-        for n in range(1, 8):
-            fin_copy(n).start()
-        f_got[dp] = f_send[dp]
+        total = total * (24576.0 ** (-0.5))
+        for n in range(8):
+            out_grad[:, n * 128 : (n + 1) * 128] = total[8 * n : 8 * n + 8]
 
     back_part(0, 0)
     back_part(0, 1)
     return_part(0, 0)
-    gate()
     back_part(1, 0)
     return_part(0, 1)
+    gate()
     back_part(1, 1)
     return_part(1, 0)
     back_part(2, 0)
     return_part(1, 1)
     back_part(2, 1)
+    back_part(3, 0)
     return_part(2, 0)
+    back_part(3, 1)
+    return_part(2, 1)
+    return_queries(1)
+    return_part(3, 0)
     product()
-    back_part(3, 0)
-    return_part(2, 1)
-    back_part(3, 1)
-    return_part(3, 0)
-    return_queries(0, 1)
-    return_queries(1, 1)
     return_part(3, 1)
 
     layer_out[...] = (dot_nn(gated_buf[...], w_out[...]) + tokens[...].astype(F32)).astype(BF16)
@@ -616,8 +653,8 @@
         grad_pre = (gradient.astype(F32) * slope_buf[:, col : col + D]).astype(BF16)
         rows_acc[...] += dot_nt(grad_pre, w_buf[:, col : col + D])
 
+    spread()
     rows_part(1, V_COL)
-    sum_places()
     rows_part(0, K_COL)
     rows_part(2, Q_COL)
 
@@ -626,9 +663,7 @@
         go_all[dp].astype(F32) + norm_back(rows_acc[...], normed, inv_x)
     ).astype(BF16)
 
-    wait_arrived(f_got.at[0:7], fin_recv)
-    for n in range(8):
-        out_grad[:, n * 128 : (n + 1) * 128] = f_got[n]
+    sum_places()
 
     for n in range(1, 4):
         go_along(n).wait_send()
@@ -698,8 +733,8 @@
             vmem((ROWS, D), F32),
             vmem((1, 256), jnp.int32),
             vmem((2, 8, 1, 256), jnp.int32),
-            vmem((2, 4, G, 128), F32),
-            vmem((2, 2, 1, G), F32),
+            vmem((2, 4, G, 128), BF16),
+            vmem((2, 2, G, 128), BF16),
             vmem((4, 2, HEADS, HALF, HEAD), BF16),
             vmem((2, 2, 8, HALF, HEAD), BF16),
             vmem((2, 2, 8, HALF, HEAD), BF16),
@@ -719,8 +754,8 @@
             vmem((2, 2, HEAD, G), BF16),
             vmem((2, 2, HEAD, G), F32),
             vmem((2, 4, G, HEAD), F32),
-            vmem((2, G, HEAD), F32),
-            vmem((2, 4, 2, 2, 2, HALF, HEAD), F32),
+            vmem((2, 2, ROWS, HEAD), F32),
+            vmem((2, 4, 2, 2, HALF, HEAD), F32),
             vmem((2, 4, 2, 2, HALF, HEAD), BF16),
             vmem((2, 4, 2, 2, HALF, HEAD), BF16),
             vmem((3, 2, 8, HALF, HEAD), BF16),
@@ -732,8 +767,8 @@
             vmem((CTX, 64, 128), F32),
             vmem((CTX, 64, 128), BF16),
             vmem((CTX - 1, 64, 128), BF16),
-            vmem((8, 8, 128), F32),
-            vmem((8, 8, 128), F32),
+            vmem((8, 128, 128), BF16),
+            vmem((8, 128, 128), BF16),
             dma((3,)), dma((8,)),
             dma, dma, dma, dma,
             dma((4, 2)), dma((4, 2, 2)), dma((2, 2, 2)), dma((2, 2, 2)),

time: 71.2 us -> 69.5 us (0.976)
  Pallas kernels: 70.4 us -> 68.7 us
    pallas_call x1, Pallas kernels: 68.4 us -> 66.7 us  [on_device(): pl.pallas_call(layer_kernel, out_shape=(jax.ShapeDtypeStruct((ROWS, D), B...]
where the time goes in v4:
time: 69.5 us; the launch traced here: 69.4 us
  Pallas kernels  68.7 us (99%)
    pallas_call x1, Pallas kernels, on_device(): pl.pallas_call(layer_kernel, out_shape=(jax.ShapeDtypeStruct((ROWS, D), B...  66.7 us
    pallas_call x1, Pallas kernels, copied(): pl.pallas_call(copy_kernel, out_shape=tuple((jax.ShapeDtypeStruct(a.shape...  2.02 us

profile of v4, /device:TPU:1, one launch (start us, length us, event | category | flops | bytes accessed | tf_op | source)
XLA Modules:
  0.0 69.4 jit_solution(5368267658055207735)
XLA Ops:
  0.6 66.7 %layer.1 = (bf16[192,1024]{1,0:T(8,128)(2,1)}, bf16[192,1024]{1,0:T(8,128)(2,1)}, f32[8,1024]{1,0:T(8,128)}) custom-call(bf16[192,1024]{1,0:T(8,128)(2,1)} %tokens_in.1, s32[1,192]{1,0:T(1,128)} %hist.1, bf16[1024,4096]{1,0:T(8,128)(2,1)} %w_in.1, bf16[1024,1024]{1,0:T(8,128)(2,1)} %w_out_in.1, bf16[192,1024]{1,0:T(8,128)(2,1)} %grad_out_in.1), custom_call_target="tpu_custom_call" | custom-call | tf_op jit(solution)/shard_map/layer/pallas_call | solution.py:716
  67.3 2.0 %results.1 = (bf16[192,1024]{1,0:T(8,128)(2,1)}, bf16[192,1024]{1,0:T(8,128)(2,1)}, f32[8,1024]{1,0:T(8,128)}) custom-call(bf16[192,1024]{1,0:T(8,128)(2,1)} %get-tuple-element.6.refs_0_, bf16[192,1024]{1,0:T(8,128)(2,1)} %get-tuple-element.7.refs_1_, f32[8,1024]{1,0:T(8,128)} %get-tuple-element.8.refs_2_), custom_call_target="tpu_custom_call" | custom-call | tf_op jit(solution)/shard_map/results/pallas_call | solution.py:701
